TPU v7x, 128 devices: a whole 4x4x4 slice. The times are simulated.
128 devices in a mesh: dap: 64 (over z_hi, y, x, core), dp: 2 (over z_lo).
Axes of the slice: x: 4, y: 4, z: 4 (z_hi: 2, z_lo: 2; z = z_hi * 2 + z_lo), core: 2. Of those that a mesh axis runs over, the one named last changes fastest.
Arguments:
- pair: bfloat16 [1536, 768, 128], P(('dp', 'dap')), parts along dimension 0, may hold values from -6 to 6
- pair_mask: int32 [1536, 768], P('dp', 'dap'), parts along dimension 0, may hold values 0 or 1
- ln_gain: float32 [128], replicated, may hold values from 0.1 to 1.9
- ln_offset: float32 [128], replicated, may hold values from -3 to 3
- bias_weight: bfloat16 [128, 4], replicated, may hold values from -14.142136 to 14.142136
- query_weight: bfloat16 [128, 128], replicated, may hold values from -2.4748737 to 2.4748737
- key_weight: bfloat16 [128, 128], replicated, may hold values from -2.4748737 to 2.4748737
- value_weight: bfloat16 [128, 128], replicated, may hold values from -0.5 to 0.5
- gate_weight: bfloat16 [128, 128], replicated, may hold values from -0.5 to 0.5
- gate_offset: float32 [128], replicated, may hold values from -4 to 4
- out_weight: bfloat16 [128, 128], replicated, may hold values from -0.5 to 0.5
- out_offset: float32 [128], replicated, may hold values from -3 to 3
Outputs:
- update: bfloat16 [1536, 768, 128], P(('dp', 'dap')), parts along dimension 0
There are 2 independent parts, one for each index of `dp`. A program takes and returns all parts, laid end to end along the dimension named above; an argument that names none is the same for every part. Nothing has to cross between parts.
All inputs are finite; a program needn't handle non-finite values. No bound on the sum of `pair_mask` on one device may be relied on, other than what follows from the above.
Results may differ from a plain program's by a relative error of at most 0.014.
The roundings to bfloat16 on the way count: a program that leaves them out, or rounds other values in their place, can miss the bound.
Values may be sent and summed in bfloat16 or wider, within the bound.
No kernel may reach another device: no remote copies, remote signals or barrier semaphores. Data moves between devices by JAX's collectives and lax.ppermute only.
A program may use at most 128 MiB of HBM per device.

v0:
```python
import jax
import jax.numpy as jnp
from jax import lax
from jax.sharding import PartitionSpec as P

NEG_BIG = 1000000000.0
EPSILON = 1e-05


def layer_norm(values_in, ln_gain, ln_offset):
    wide = values_in.astype(jnp.float32)
    centre = jnp.mean(wide, axis=-1, keepdims=True)
    spread = jnp.mean((wide - centre) ** 2, axis=-1, keepdims=True)
    return (wide - centre) * lax.rsqrt(spread + EPSILON) * ln_gain + ln_offset


def local(
    pair,
    pair_mask,
    ln_gain,
    ln_offset,
    bias_weight,
    query_weight,
    key_weight,
    value_weight,
    gate_weight,
    gate_offset,
    out_weight,
    out_offset,
):
    row_count, pair_width, channels = pair.shape
    groups = lax.axis_size("dap")
    col_count = pair_width // groups
    head_count = bias_weight.shape[1]
    head_dim = channels // head_count
    normed = layer_norm(pair, ln_gain, ln_offset).astype(jnp.bfloat16)
    bias_local = jnp.einsum(
        "rnc,ch->hrn", normed, bias_weight, preferred_element_type=jnp.float32
    ).astype(jnp.bfloat16)
    split_shape = (row_count, groups, col_count, channels)
    column_shape = (pair_width, col_count, channels)
    moved = lax.all_to_all(
        normed.reshape(split_shape), "dap", split_axis=1, concat_axis=0, tiled=True
    )
    source = moved.reshape(pair_width * col_count, channels)
    query = (
        jnp.dot(source, query_weight, preferred_element_type=jnp.float32) * head_dim ** (-0.5)
    ).astype(jnp.bfloat16)
    keys_all = jnp.dot(source, key_weight, preferred_element_type=jnp.float32).astype(jnp.bfloat16)
    values_all = jnp.dot(source, value_weight, preferred_element_type=jnp.float32).astype(
        jnp.bfloat16
    )
    gate = jax.nn.sigmoid(
        jnp.dot(source, gate_weight, preferred_element_type=jnp.float32) + gate_offset
    ).astype(jnp.bfloat16)
    query, keys_all, values_all, gate = tuple(
        (item.reshape(column_shape) for item in (query, keys_all, values_all, gate))
    )
    heads_shape = (pair_width, col_count, head_count, head_dim)
    query_cols = jnp.transpose(query.reshape(heads_shape), (1, 0, 2, 3))
    key_cols = jnp.transpose(keys_all.reshape(heads_shape), (1, 0, 2, 3))
    value_cols = jnp.transpose(values_all.reshape(heads_shape), (1, 0, 2, 3))
    mask_cols = jnp.transpose(pair_mask)
    whole_bias = lax.all_gather(bias_local, "dap", axis=1, tiled=True)
    bias_wide = whole_bias.astype(jnp.float32)

    def per_column(column_args):
        query_one, key_one, value_one, mask_one = column_args
        scores = jnp.einsum("ihd,khd->hki", query_one, key_one, preferred_element_type=jnp.float32)
        scores = scores + bias_wide + NEG_BIG * (mask_one.astype(jnp.float32) - 1.0)[None, :, None]
        top = jnp.max(scores, axis=1)
        probs = jnp.exp(scores - top[:, None, :])
        totals = jnp.sum(probs, axis=1)
        weighted = jnp.einsum(
            "hki,khd->hid",
            probs.astype(jnp.bfloat16),
            value_one,
            preferred_element_type=jnp.float32,
        )
        return (top, totals, weighted)

    top, totals, weighted = lax.map(per_column, (query_cols, key_cols, value_cols, mask_cols))
    attended = weighted / totals[..., None]
    attended = jnp.transpose(attended, (2, 0, 1, 3)).reshape(column_shape)
    gated = (attended * gate.astype(jnp.float32)).astype(jnp.bfloat16)
    returned = lax.all_to_all(
        gated.reshape(pair_width, 1, col_count, channels),
        "dap",
        split_axis=0,
        concat_axis=1,
        tiled=True,
    )
    returned = returned.reshape(row_count * pair_width, channels)
    update = jnp.dot(returned, out_weight, preferred_element_type=jnp.float32) + out_offset
    return update.astype(jnp.bfloat16).reshape(row_count, pair_width, channels)


def solution(mesh):
    in_specs = (
        P(("dp", "dap"), None, None),
        P("dp", "dap"),
        P(),
        P(),
        P(),
        P(),
        P(),
        P(),
        P(),
        P(),
        P(),
        P(),
    )
    out_specs = P(("dp", "dap"), None, None)
    return jax.shard_map(local, mesh=mesh, in_specs=in_specs, out_specs=out_specs, check_vma=False)
```

profile of v0, /device:TPU:1, one launch (start us, length us, event | category | flops | bytes accessed | tf_op | source)
XLA Modules:
  0.0 406.5 jit_solution(14931095841032777791)
XLA Ops:
  6.6 2.5 convert_reduce_fusion
  9.1 4.1 %fusion.29 = f32[12,768]{1,0:T(8,128)S(1)} fusion(bf16[12,768,128]{2,1,0:T(8,128)(2,1)} %param.14, f32[12,768]{1,0:T(8,128)S(1)} %broadcast_multiply_fusion), kind=kLoop, calls=%fused_computation.35 | loop fusion | flops 4709376 | bytes 2433024 | tf_op jit(solution)/shard_map/reduce_sum | solution.py:13
  13.3 2.9 fusion.32
  16.2 1.4 copy-done.3
  17.6 1.3 fusion.34
  19.0 3.5 reshape.78
  22.5 2.6 copy.40
  25.1 12.3 %all-to-all-start = ((bf16[12,64,12,128]{3,2,0,1:T(8,128)(2,1)}), bf16[12,64,12,128]{3,2,0,1:T(8,128)(2,1)S(1)}, u32[]{:S(2)}, u32[]{:S(2)}) async-start(bf16[12,64,12,128]{3,2,0,1:T(8,128)(2,1)} %copy.40), calls=%async_computation | async-start | bytes 6291456 | tf_op jit(solution)/shard_map/all_to_all | solution.py:42
  37.4 42.5 %all-to-all-done = bf16[12,64,12,128]{3,2,0,1:T(8,128)(2,1)S(1)} async-done(((bf16[12,64,12,128]{3,2,0,1:T(8,128)(2,1)}), bf16[12,64,12,128]{3,2,0,1:T(8,128)(2,1)S(1)}, u32[]{:S(2)}, u32[]{:S(2)}) %all-to-all-start) | async-done | bytes 2359328 | tf_op jit(solution)/shard_map/all_to_all | solution.py:42
  79.9 1.6 copy-done.5
  81.5 3.7 reshape.79
  85.2 2.2 convolution_convert_fusion.1
  87.4 13.0 %reshape_reshape.9 = bf16[768,12,4,32]{3,2,1,0:T(4,128)(2,1)} reshape(bf16[9216,128]{1,0:T(8,128)(2,1)} %convolution_convert_fusion.1) | data formatting | bytes 4718592 | tf_op jit(solution)/shard_map/reshape;reshape | solution.py:61
  100.4 14.3 %copy.41 = bf16[12,768,4,32]{1,3,2,0:T(8,128)(2,1)} copy(bf16[12,768,4,32]{3,2,0,1:T(4,128)(2,1)} %bitcast.67) | data formatting | bytes 4718592 | tf_op jit(solution)/shard_map/while | solution.py:82
  114.8 2.2 fusion.22
  116.9 13.0 %reshape_reshape.10 = bf16[768,12,4,32]{3,2,1,0:T(4,128)(2,1)} reshape(bf16[9216,128]{1,0:T(8,128)(2,1)} %fusion.22) | data formatting | bytes 4718592 | tf_op jit(solution)/shard_map/reshape;reshape | solution.py:60
  129.9 14.2 %copy.42 = bf16[12,768,4,32]{1,3,2,0:T(8,128)(2,1)} copy(bf16[12,768,4,32]{3,2,0,1:T(4,128)(2,1)} %bitcast.68) | data formatting | bytes 4718592 | tf_op jit(solution)/shard_map/while | solution.py:82
  144.2 2.1 convolution_convert_fusion
  146.3 13.0 %reshape_reshape.11 = bf16[768,12,4,32]{3,2,1,0:T(4,128)(2,1)} reshape(bf16[9216,128]{1,0:T(8,128)(2,1)} %convolution_convert_fusion) | data formatting | bytes 4718592 | tf_op jit(solution)/shard_map/reshape;reshape | solution.py:62
  159.3 14.2 %copy.44 = bf16[12,768,4,32]{1,3,2,0:T(8,128)(2,1)} copy(bf16[12,768,4,32]{3,2,0,1:T(4,128)(2,1)} %bitcast.69) | data formatting | bytes 4718592 | tf_op jit(solution)/shard_map/while | solution.py:82
  173.6 3.6 fusion.26
  177.2 6.4 %reshape.83 = f32[768,1,12,128]{3,2,0,1:T(8,128)} reshape(f32[9216,128]{1,0:T(8,128)} %fusion.26) | data formatting | bytes 9437184 | tf_op jit(solution)/shard_map/convert_element_type | solution.py:85
  183.6 6.3 %copy.45 = f32[768,1,12,128]{0,3,2,1:T(8,128)} copy(f32[768,1,12,128]{3,2,0,1:T(8,128)} %reshape.83) | data formatting | bytes 9437184 | tf_op jit(solution)/shard_map/convert_element_type | solution.py:85
  190.0 6.7 %copy.43 = f32[4,768,768]{2,1,0:T(8,128)} copy(bf16[4,768,768]{2,0,1:T(4,128)(2,1)} %all-gather.2.cloned.1.call-done) | data formatting | bytes 14155776 | tf_op jit(solution)/shard_map/while | solution.py:82
  196.7 132.7 %while.14 = (s32[]{:T(128)}, f32[12,4,768]{2,1,0:T(4,128)S(1)}, f32[12,4,768,32]{2,3,1,0:T(8,128)}, bf16[12,768,4,32]{1,3,2,0:T(8,128)(2,1)}, bf16[12,768,4,32]{...) while((s32[]{:T(128)}, f32[12,4,768]{2,1,0:T(4,128)S(1)}, ...), condition=%wide.region_5.6_spmd, body=%wide.region_2.5_spmd.sunk | while | flops 318501120 | bytes 38816868 | solution.py:82
  197.5 5.8 %fusion.55 = (f32[4,768]{1,0:T(4,128)S(1)}, f32[4,768,768]{2,1,0:T(8,128)S(1)}) fusion(f32[768]{0:T(1024)S(1)} %multiply_reduce_fusion.2, f32[4,768,768]{2,1,0:T(8,128)} %get-tuple-element.243, bf16[12,768,4,32]{1,3,2,0:T(8,128)(2,1)} %get-tuple-element.242, s32[]{:T(128)} %get-tuple-element.229, bf16[12,768,4,32]{1,3,2,0:T(8,128)(2,1)} %get-tuple-element.241), kind=kOutput, calls=%fused_computation.48.clone.1 | convolution fusion | flops 158069760 | bytes 19283968 | tf_op jit(solution)/shard_map/while/body/eval_jaxpr/ihd,khd->hki/dot_general | solution.py:69
  203.2 3.2 fusion.57
  206.5 1.3 fusion.56
  208.5 5.8 %fusion.55 = (f32[4,768]{1,0:T(4,128)S(1)}, f32[4,768,768]{2,1,0:T(8,128)S(1)}) fusion(f32[768]{0:T(1024)S(1)} %multiply_reduce_fusion.2, f32[4,768,768]{2,1,0:T(8,128)} %get-tuple-element.243, bf16[12,768,4,32]{1,3,2,0:T(8,128)(2,1)} %get-tuple-element.242, s32[]{:T(128)} %get-tuple-element.229, bf16[12,768,4,32]{1,3,2,0:T(8,128)(2,1)} %get-tuple-element.241), kind=kOutput, calls=%fused_computation.48.clone.1 | convolution fusion | flops 158069760 | bytes 19283968 | tf_op jit(solution)/shard_map/while/body/eval_jaxpr/ihd,khd->hki/dot_general | solution.py:69
  214.3 3.3 fusion.57
  217.6 1.3 fusion.56
  219.6 5.8 %fusion.55 = (f32[4,768]{1,0:T(4,128)S(1)}, f32[4,768,768]{2,1,0:T(8,128)S(1)}) fusion(f32[768]{0:T(1024)S(1)} %multiply_reduce_fusion.2, f32[4,768,768]{2,1,0:T(8,128)} %get-tuple-element.243, bf16[12,768,4,32]{1,3,2,0:T(8,128)(2,1)} %get-tuple-element.242, s32[]{:T(128)} %get-tuple-element.229, bf16[12,768,4,32]{1,3,2,0:T(8,128)(2,1)} %get-tuple-element.241), kind=kOutput, calls=%fused_computation.48.clone.1 | convolution fusion | flops 158069760 | bytes 19283968 | tf_op jit(solution)/shard_map/while/body/eval_jaxpr/ihd,khd->hki/dot_general | solution.py:69
  225.4 3.2 fusion.57
  228.6 1.3 fusion.56
  230.7 5.8 %fusion.55 = (f32[4,768]{1,0:T(4,128)S(1)}, f32[4,768,768]{2,1,0:T(8,128)S(1)}) fusion(f32[768]{0:T(1024)S(1)} %multiply_reduce_fusion.2, f32[4,768,768]{2,1,0:T(8,128)} %get-tuple-element.243, bf16[12,768,4,32]{1,3,2,0:T(8,128)(2,1)} %get-tuple-element.242, s32[]{:T(128)} %get-tuple-element.229, bf16[12,768,4,32]{1,3,2,0:T(8,128)(2,1)} %get-tuple-element.241), kind=kOutput, calls=%fused_computation.48.clone.1 | convolution fusion | flops 158069760 | bytes 19283968 | tf_op jit(solution)/shard_map/while/body/eval_jaxpr/ihd,khd->hki/dot_general | solution.py:69
  236.4 3.2 fusion.57
  239.7 1.3 fusion.56
  241.7 5.8 %fusion.55 = (f32[4,768]{1,0:T(4,128)S(1)}, f32[4,768,768]{2,1,0:T(8,128)S(1)}) fusion(f32[768]{0:T(1024)S(1)} %multiply_reduce_fusion.2, f32[4,768,768]{2,1,0:T(8,128)} %get-tuple-element.243, bf16[12,768,4,32]{1,3,2,0:T(8,128)(2,1)} %get-tuple-element.242, s32[]{:T(128)} %get-tuple-element.229, bf16[12,768,4,32]{1,3,2,0:T(8,128)(2,1)} %get-tuple-element.241), kind=kOutput, calls=%fused_computation.48.clone.1 | convolution fusion | flops 158069760 | bytes 19283968 | tf_op jit(solution)/shard_map/while/body/eval_jaxpr/ihd,khd->hki/dot_general | solution.py:69
  247.5 3.2 fusion.57
  250.7 1.3 fusion.56
  252.8 5.8 %fusion.55 = (f32[4,768]{1,0:T(4,128)S(1)}, f32[4,768,768]{2,1,0:T(8,128)S(1)}) fusion(f32[768]{0:T(1024)S(1)} %multiply_reduce_fusion.2, f32[4,768,768]{2,1,0:T(8,128)} %get-tuple-element.243, bf16[12,768,4,32]{1,3,2,0:T(8,128)(2,1)} %get-tuple-element.242, s32[]{:T(128)} %get-tuple-element.229, bf16[12,768,4,32]{1,3,2,0:T(8,128)(2,1)} %get-tuple-element.241), kind=kOutput, calls=%fused_computation.48.clone.1 | convolution fusion | flops 158069760 | bytes 19283968 | tf_op jit(solution)/shard_map/while/body/eval_jaxpr/ihd,khd->hki/dot_general | solution.py:69
  258.5 3.2 fusion.57
  261.8 1.3 fusion.56
  263.8 5.8 %fusion.55 = (f32[4,768]{1,0:T(4,128)S(1)}, f32[4,768,768]{2,1,0:T(8,128)S(1)}) fusion(f32[768]{0:T(1024)S(1)} %multiply_reduce_fusion.2, f32[4,768,768]{2,1,0:T(8,128)} %get-tuple-element.243, bf16[12,768,4,32]{1,3,2,0:T(8,128)(2,1)} %get-tuple-element.242, s32[]{:T(128)} %get-tuple-element.229, bf16[12,768,4,32]{1,3,2,0:T(8,128)(2,1)} %get-tuple-element.241), kind=kOutput, calls=%fused_computation.48.clone.1 | convolution fusion | flops 158069760 | bytes 19283968 | tf_op jit(solution)/shard_map/while/body/eval_jaxpr/ihd,khd->hki/dot_general | solution.py:69
  269.6 3.2 fusion.57
  272.8 1.3 fusion.56
  274.9 5.8 %fusion.55 = (f32[4,768]{1,0:T(4,128)S(1)}, f32[4,768,768]{2,1,0:T(8,128)S(1)}) fusion(f32[768]{0:T(1024)S(1)} %multiply_reduce_fusion.2, f32[4,768,768]{2,1,0:T(8,128)} %get-tuple-element.243, bf16[12,768,4,32]{1,3,2,0:T(8,128)(2,1)} %get-tuple-element.242, s32[]{:T(128)} %get-tuple-element.229, bf16[12,768,4,32]{1,3,2,0:T(8,128)(2,1)} %get-tuple-element.241), kind=kOutput, calls=%fused_computation.48.clone.1 | convolution fusion | flops 158069760 | bytes 19283968 | tf_op jit(solution)/shard_map/while/body/eval_jaxpr/ihd,khd->hki/dot_general | solution.py:69
  280.7 3.2 fusion.57
  286.0 5.8 %fusion.55 = (f32[4,768]{1,0:T(4,128)S(1)}, f32[4,768,768]{2,1,0:T(8,128)S(1)}) fusion(f32[768]{0:T(1024)S(1)} %multiply_reduce_fusion.2, f32[4,768,768]{2,1,0:T(8,128)} %get-tuple-element.243, bf16[12,768,4,32]{1,3,2,0:T(8,128)(2,1)} %get-tuple-element.242, s32[]{:T(128)} %get-tuple-element.229, bf16[12,768,4,32]{1,3,2,0:T(8,128)(2,1)} %get-tuple-element.241), kind=kOutput, calls=%fused_computation.48.clone.1 | convolution fusion | flops 158069760 | bytes 19283968 | tf_op jit(solution)/shard_map/while/body/eval_jaxpr/ihd,khd->hki/dot_general | solution.py:69
  291.7 3.2 fusion.57
  297.0 5.8 %fusion.55 = (f32[4,768]{1,0:T(4,128)S(1)}, f32[4,768,768]{2,1,0:T(8,128)S(1)}) fusion(f32[768]{0:T(1024)S(1)} %multiply_reduce_fusion.2, f32[4,768,768]{2,1,0:T(8,128)} %get-tuple-element.243, bf16[12,768,4,32]{1,3,2,0:T(8,128)(2,1)} %get-tuple-element.242, s32[]{:T(128)} %get-tuple-element.229, bf16[12,768,4,32]{1,3,2,0:T(8,128)(2,1)} %get-tuple-element.241), kind=kOutput, calls=%fused_computation.48.clone.1 | convolution fusion | flops 158069760 | bytes 19283968 | tf_op jit(solution)/shard_map/while/body/eval_jaxpr/ihd,khd->hki/dot_general | solution.py:69
  302.8 3.2 fusion.57
  308.1 5.8 %fusion.55 = (f32[4,768]{1,0:T(4,128)S(1)}, f32[4,768,768]{2,1,0:T(8,128)S(1)}) fusion(f32[768]{0:T(1024)S(1)} %multiply_reduce_fusion.2, f32[4,768,768]{2,1,0:T(8,128)} %get-tuple-element.243, bf16[12,768,4,32]{1,3,2,0:T(8,128)(2,1)} %get-tuple-element.242, s32[]{:T(128)} %get-tuple-element.229, bf16[12,768,4,32]{1,3,2,0:T(8,128)(2,1)} %get-tuple-element.241), kind=kOutput, calls=%fused_computation.48.clone.1 | convolution fusion | flops 158069760 | bytes 19283968 | tf_op jit(solution)/shard_map/while/body/eval_jaxpr/ihd,khd->hki/dot_general | solution.py:69
  313.8 3.3 fusion.57
  317.1 1.3 fusion.56
  319.1 5.8 %fusion.55 = (f32[4,768]{1,0:T(4,128)S(1)}, f32[4,768,768]{2,1,0:T(8,128)S(1)}) fusion(f32[768]{0:T(1024)S(1)} %multiply_reduce_fusion.2, f32[4,768,768]{2,1,0:T(8,128)} %get-tuple-element.243, bf16[12,768,4,32]{1,3,2,0:T(8,128)(2,1)} %get-tuple-element.242, s32[]{:T(128)} %get-tuple-element.229, bf16[12,768,4,32]{1,3,2,0:T(8,128)(2,1)} %get-tuple-element.241), kind=kOutput, calls=%fused_computation.48.clone.1 | convolution fusion | flops 158069760 | bytes 19283968 | tf_op jit(solution)/shard_map/while/body/eval_jaxpr/ihd,khd->hki/dot_general | solution.py:69
  324.9 3.2 fusion.57
  329.4 3.0 broadcast_divide_fusion
  333.2 2.2 fusion.33
  335.4 4.0 copy.46
  339.4 50.3 %all_to_all.30 = bf16[768,1,12,128]{3,2,1,0:T(8,128)(2,1)S(1)} all-to-all(bf16[768,1,12,128]{3,2,1,0:T(8,128)(2,1)S(1)} %copy.46), channel_id=1, replica_groups=mesh['dap'=64,'dp'=2] {'dap'}, dimensions={0} | all-to-all | bytes 4718592 | tf_op jit(solution)/shard_map/all_to_all | solution.py:86
  390.5 3.3 copy.48
  393.8 3.7 reshape.81
  397.5 2.2 fusion.23
  (64 shorter events, 15.9 us)
Async XLA Ops:
  6.5 78.7 %copy-start = (bf16[128,128]{1,0:T(8,128)(2,1)S(1)}, bf16[128,128]{1,0:T(8,128)(2,1)}, u32[]{:S(2)}) copy-start(bf16[128,128]{1,0:T(8,128)(2,1)} %param.20) | copy-start | bytes 98308
  6.5 6.7 %copy-start.2 = (bf16[12,768,128]{2,1,0:T(8,128)(2,1)S(1)}, bf16[12,768,128]{2,1,0:T(8,128)(2,1)}, u32[]{:S(2)}) copy-start(bf16[12,768,128]{2,1,0:T(8,128)(2,1)} %param.14) | copy-start | bytes 7077892
  6.5 6.7 %copy-start.12 = (f32[128]{0:T(128)S(1)}, f32[128]{0:T(128)}, u32[]{:S(2)}) copy-start(f32[128]{0:T(128)} %param.16) | copy-start | bytes 1540
  6.5 6.7 %copy-start.11 = (f32[128]{0:T(128)S(1)}, f32[128]{0:T(128)}, u32[]{:S(2)}) copy-start(f32[128]{0:T(128)} %param.17) | copy-start | bytes 1540
  6.5 11.1 %copy-start.10 = (bf16[128,4]{0,1:T(4,128)(2,1)S(1)}, bf16[128,4]{0,1:T(4,128)(2,1)}, u32[]{:S(2)}) copy-start(bf16[128,4]{0,1:T(4,128)(2,1)} %param.18) | copy-start | bytes 3076
  6.5 183.4 %all-gather.2.cloned.1.call-start = ((), (), s32[]{:S(2)}) async-start(), calls=%async_computation.2 | async-start | bytes 4792320 | tf_op jit(solution)/shard_map/all_gather | solution.py:64
  16.2 1.4 copy-start.3
  25.1 54.8 %all-to-all-start = ((bf16[12,64,12,128]{3,2,0,1:T(8,128)(2,1)}), bf16[12,64,12,128]{3,2,0,1:T(8,128)(2,1)S(1)}, u32[]{:S(2)}, u32[]{:S(2)}) async-start(bf16[12,64,12,128]{3,2,0,1:T(8,128)(2,1)} %copy.40), calls=%async_computation | async-start | bytes 6291456 | tf_op jit(solution)/shard_map/all_to_all | solution.py:42
  79.9 1.6 copy-start.5
  100.4 14.3 %copy-start.6 = (bf16[128,128]{1,0:T(8,128)(2,1)S(1)}, bf16[128,128]{1,0:T(8,128)(2,1)}, u32[]{:S(2)}) copy-start(bf16[128,128]{1,0:T(8,128)(2,1)} %param.19) | copy-start | bytes 98308
  129.9 14.2 %copy-start.7 = (bf16[128,128]{1,0:T(8,128)(2,1)S(1)}, bf16[128,128]{1,0:T(8,128)(2,1)}, u32[]{:S(2)}) copy-start(bf16[128,128]{1,0:T(8,128)(2,1)} %param.21) | copy-start | bytes 98308
  159.3 14.2 %copy-start.13 = (bf16[128,128]{1,0:T(8,128)(2,1)S(1)}, bf16[128,128]{1,0:T(8,128)(2,1)}, u32[]{:S(2)}) copy-start(bf16[128,128]{1,0:T(8,128)(2,1)} %param.22) | copy-start | bytes 98308
  159.3 14.2 %copy-start.14 = (f32[128]{0:T(128)S(1)}, f32[128]{0:T(128)}, u32[]{:S(2)}) copy-start(f32[128]{0:T(128)} %param.23) | copy-start | bytes 1540
  329.4 3.8 copy-start.4
  390.5 7.0 %copy-start.8 = (bf16[128,128]{1,0:T(8,128)(2,1)S(1)}, bf16[128,128]{1,0:T(8,128)(2,1)}, u32[]{:S(2)}) copy-start(bf16[128,128]{1,0:T(8,128)(2,1)} %param.24) | copy-start | bytes 98308
  390.5 7.0 %copy-start.9 = (f32[128]{0:T(128)S(1)}, f32[128]{0:T(128)}, u32[]{:S(2)}) copy-start(f32[128]{0:T(128)} %param.25) | copy-start | bytes 1540
  393.8 5.9 %copy-start.1 = (bf16[128,128]{1,0:T(8,128)(2,1)S(1)}, bf16[128,128]{1,0:T(8,128)(2,1)}, u32[]{:S(2)}) copy-start(bf16[128,128]{1,0:T(8,128)(2,1)} %param.20) | copy-start | bytes 98308
Sparse Core Ops, SparseCore 0:
  19.1 98.7 all-gather.1
where the time goes:
time: 410 us; the launch traced here: 406 us
  local copies, waits for them, and re-layouts  127 us (31%)
  matrix products  122 us (30%)
  blocking collectives  50.3 us (12%)
  waiting for transfers between devices  42.5 us (10%)
  other arithmetic  38.9 us (9%)
  between operations  13.6 us (3%)
  starting transfers between devices  12.3 us (3%)
    dot_general x12, matrix products, per_column(): jnp.einsum('ihd,khd->hki', query_one, key_one, preferred_element_type=jnp...  69.1 us
    all_to_all x1, blocking collectives, local(): lax.all_to_all(gated.reshape(pair_width, 1, col_count, channels), 'dap',...  50.3 us
    while x4, local copies, waits for them, and re-layouts, local(): lax.map(per_column, (query_cols, key_cols, value_cols, mask_cols))  49.5 us
    all_to_all x1, waiting for transfers between devices, local(): lax.all_to_all(normed.reshape(split_shape), 'dap', split_axis=1, concat_a...  42.5 us
    dot_general x12, matrix products, per_column(): jnp.einsum('hki,khd->hid', probs.astype(jnp.bfloat16), value_one, preferr...  38.9 us
    convert_element_type x3, local copies, waits for them, and re-layouts, local(): gated = (attended * gate.astype(jnp.float32)).astype(jnp.bfloat16)  16.8 us
    reduce_sum x12, other arithmetic, per_column(): totals = jnp.sum(probs, axis=1)  15.1 us
    another operation x1, local copies, waits for them, and re-layouts, local(): key_cols = jnp.transpose(keys_all.reshape(heads_shape), (1, 0, 2, 3))  13 us
  transfers between devices with their start and end apart: 2, of which 1 were waited for; matrix products, arithmetic and copies ran while one was open for 28% of the time, Pallas kernels for 0%

commit v1 on v0

v1 whole, which is shorter than its diff:
```python
import functools

import jax
import jax.numpy as jnp
from jax import lax
from jax.experimental import pallas as pl
from jax.experimental.pallas import tpu as pltpu
from jax.sharding import PartitionSpec as P

NEG_BIG = 1000000000.0
EPSILON = 1e-05
CHUNKS = 2
TOTAL_LOW = 1e-20
TOTAL_HIGH = 1e30
NT = (((1,), (1,)), ((), ()))


def dot(lhs, rhs):
    return jnp.dot(lhs, rhs, preferred_element_type=jnp.float32)


def dot_nt(lhs, rhs):
    return lax.dot_general(lhs, rhs, NT, preferred_element_type=jnp.float32)


def in_vmem(count):
    return [pl.BlockSpec(memory_space=pltpu.VMEM)] * count


def prepare_kernel(rows, width, groups, chunks, heads, pair_ref, gain_ref, offset_ref, bias_weight_ref, *refs):
    chunk_refs, bias_ref = refs[:chunks], refs[chunks]
    normed_ref, bias_wide_ref = refs[chunks + 1], refs[chunks + 2]
    staged_refs = refs[chunks + 3 :]
    cols = width // groups
    per = cols // chunks
    channels = pair_ref.shape[1]
    average = jnp.full((2 * channels, channels), 1.0 / channels, jnp.bfloat16)
    weight = bias_weight_ref[...].astype(jnp.float32).T.astype(jnp.bfloat16)
    for row in range(rows):
        block = pair_ref[pl.ds(row * width, width), :]
        wide = block.astype(jnp.float32)
        centred = wide - dot(block, average[:channels])
        square = centred * centred
        high = square.astype(jnp.bfloat16)
        low = (square - high.astype(jnp.float32)).astype(jnp.bfloat16)
        spread = dot(jnp.concatenate([high, low], axis=1), average)
        normed = (centred * lax.rsqrt(spread + EPSILON) * gain_ref[...] + offset_ref[...]).astype(jnp.bfloat16)
        normed_ref[pl.ds(row * width, width), :] = normed.astype(jnp.float32)
        bias_wide_ref[pl.ds(row * heads, heads), :] = dot_nt(weight, normed)
        for col in range(cols):
            chunk, place = divmod(col, per)
            staged_refs[chunk][pl.ds(row * per + place, groups, stride=rows * per), :] = normed_ref[
                pl.ds(row * width + col, groups, stride=cols), :
            ]
    for chunk in range(chunks):
        chunk_refs[chunk][...] = staged_refs[chunk][...].astype(jnp.bfloat16)
    bias_ref[...] = bias_wide_ref[...].astype(jnp.bfloat16)


def turn_kernel(heads, gathered_ref, turned_ref, wide_ref):
    width = gathered_ref.shape[1]
    tile = wide_ref.shape[2]
    for at in range(0, width, tile):
        wide_ref[at // tile] = gathered_ref[:, at : at + tile].astype(jnp.float32)
    unit = (
        lax.broadcasted_iota(jnp.int32, (tile, tile), 0) == lax.broadcasted_iota(jnp.int32, (tile, tile), 1)
    ).astype(jnp.bfloat16)
    for head in range(heads):
        for at in range(0, width, tile):
            one = wide_ref[at // tile, pl.ds(head, width, stride=heads), :].astype(jnp.bfloat16)
            turned_ref[head, pl.ds(at, tile), :] = dot_nt(unit, one).astype(jnp.bfloat16)


def attend_kernel(
    chunk,
    per,
    heads,
    moved_ref,
    bias_ref,
    mask_ref,
    query_weight_ref,
    key_weight_ref,
    value_weight_ref,
    gate_weight_ref,
    gate_offset_ref,
    out_ref,
    source_ref,
    weight_ref,
    key_ref,
    value_ref,
    result_ref,
    fine_ref,
):
    channels = moved_ref.shape[1]
    width = mask_ref.shape[0]
    mask_cols = mask_ref.shape[1]
    head_dim = channels // heads
    source_ref[...] = moved_ref[...].astype(jnp.float32)
    for at, ref in enumerate((query_weight_ref, key_weight_ref, value_weight_ref, gate_weight_ref)):
        weight_ref[:, at * channels : (at + 1) * channels] = ref[...]
    lane_head = lax.broadcasted_iota(jnp.int32, (1, channels), 1) // head_dim
    own = [(lane_head == head).astype(jnp.bfloat16) for head in range(heads)]
    fine_ref[...] = jnp.ones_like(fine_ref)

    def project(col):
        source = source_ref[pl.ds(col, width, stride=per), :].astype(jnp.bfloat16)
        wide = dot(source, weight_ref[...])
        query = (wide[:, :channels] * head_dim ** (-0.5)).astype(jnp.bfloat16)
        keys = wide[:, channels : 2 * channels].astype(jnp.bfloat16)
        values = wide[:, 2 * channels : 3 * channels].astype(jnp.bfloat16)
        gate = jax.nn.sigmoid(wide[:, 3 * channels :] + gate_offset_ref[...]).astype(jnp.bfloat16)
        pick = (lax.broadcasted_iota(jnp.int32, (mask_cols, channels), 0) == chunk * per + col).astype(jnp.bfloat16)
        present = dot(mask_ref[...].astype(jnp.float32).astype(jnp.bfloat16), pick).astype(jnp.bfloat16)
        for head in range(heads):
            key_ref[head] = keys * own[head]
        return query, values, gate.astype(jnp.float32), present

    def column(col, carry):
        query, values, gate, present = project(col)
        shown = values * present
        for head in range(heads):
            value_ref[head, :, :channels] = shown * own[head]
            value_ref[head, :, channels:] = present * own[head]
        total = jnp.zeros((width, 2 * channels), jnp.float32)
        for head in range(heads):
            scores = dot_nt(query, key_ref[head]) + bias_ref[head].astype(jnp.float32)
            total += dot(jnp.exp(scores).astype(jnp.bfloat16), value_ref[head])
        sums = total[:, channels:]
        fine = jnp.where((sums > TOTAL_LOW) & (sums < TOTAL_HIGH), 1.0, 0.0)
        fine_ref[...] = jnp.minimum(fine_ref[...], jnp.min(fine.reshape(width // 8, 8, channels), axis=0))
        result_ref[pl.ds(col, width, stride=per), :] = total[:, :channels] / sums * gate
        return carry

    lax.fori_loop(0, per, column, 0)

    @pl.when(jnp.min(fine_ref[...]) < 0.5)
    def _():
        tile = 128

        def exact(col, carry):
            query, values, gate, present = project(col)
            first = (lax.broadcasted_iota(jnp.int32, (8, channels), 1) == 0).astype(jnp.bfloat16)
            lift = NEG_BIG * (dot_nt(first, present)[:1] - 1.0)
            for head in range(heads):
                value_ref[head, :, :channels] = values * own[head]
            parts = []
            for at in range(0, width, tile):
                attended = jnp.zeros((tile, channels), jnp.float32)
                for head in range(heads):
                    scores = dot_nt(query[at : at + tile], key_ref[head])
                    scores = scores + bias_ref[head, at : at + tile, :].astype(jnp.float32) + lift
                    probs = jnp.exp(scores - jnp.max(scores, axis=1, keepdims=True))
                    totals = jnp.sum(probs, axis=1, keepdims=True)
                    attended += dot(probs.astype(jnp.bfloat16), value_ref[head, :, :channels]) / totals
                parts.append(attended)
            result_ref[pl.ds(col, width, stride=per), :] = jnp.concatenate(parts, axis=0) * gate
            return carry

        lax.fori_loop(0, per, exact, 0)

    out_ref[...] = result_ref[...].astype(jnp.bfloat16)


def finish_kernel(rows, width, groups, chunks, *refs):
    chunk_refs = refs[:chunks]
    out_weight_ref, out_offset_ref, update_ref = refs[chunks : chunks + 3]
    wide_refs = refs[chunks + 3 : 2 * chunks + 3]
    row_ref = refs[2 * chunks + 3]
    cols = width // groups
    per = cols // chunks
    for chunk in range(chunks):
        wide_refs[chunk][...] = dot(chunk_refs[chunk][...], out_weight_ref[...]) + out_offset_ref[...]
    for row in range(rows):
        for col in range(cols):
            chunk, place = divmod(col, per)
            row_ref[row % 2, pl.ds(col, groups, stride=cols), :] = wide_refs[chunk][
                pl.ds(row * per + place, groups, stride=rows * per), :
            ]
        update_ref[pl.ds(row * width, width), :] = row_ref[row % 2].astype(jnp.bfloat16)


def local(
    pair,
    pair_mask,
    ln_gain,
    ln_offset,
    bias_weight,
    query_weight,
    key_weight,
    value_weight,
    gate_weight,
    gate_offset,
    out_weight,
    out_offset,
):
    rows, width, channels = pair.shape
    groups = lax.axis_size("dap")
    cols = width // groups
    per = cols // CHUNKS
    heads = bias_weight.shape[1]
    block = groups * rows * per
    low, wide = jnp.bfloat16, jnp.float32
    params = pltpu.CompilerParams(vmem_limit_bytes=56 * 1024 * 1024)
    *sends, bias_local = pl.pallas_call(
        functools.partial(prepare_kernel, rows, width, groups, CHUNKS, heads),
        out_shape=[jax.ShapeDtypeStruct((block, channels), low)] * CHUNKS
        + [jax.ShapeDtypeStruct((rows * heads, width), low)],
        in_specs=in_vmem(4),
        out_specs=in_vmem(CHUNKS + 1),
        scratch_shapes=[pltpu.VMEM((rows * width, channels), wide), pltpu.VMEM((rows * heads, width), wide)]
        + [pltpu.VMEM((block, channels), wide)] * CHUNKS,
        compiler_params=params,
        name="prepare",
    )(pair.reshape(rows * width, channels), ln_gain.reshape(1, channels), ln_offset.reshape(1, channels), bias_weight)

    gathered = lax.all_gather(bias_local, "dap", axis=0, tiled=True)
    moved = [
        lax.all_to_all(
            send.reshape(groups, rows * per, channels), "dap", split_axis=0, concat_axis=0, tiled=True
        ).reshape(block, channels)
        for send in sends
    ]
    turned = pl.pallas_call(
        functools.partial(turn_kernel, heads),
        out_shape=jax.ShapeDtypeStruct((heads, width, width), low),
        in_specs=in_vmem(1),
        out_specs=in_vmem(1)[0],
        scratch_shapes=[pltpu.VMEM((width // channels, width * heads, channels), wide)],
        compiler_params=params,
        name="turn",
    )(gathered)

    returned = []
    for chunk in range(CHUNKS):
        gated = pl.pallas_call(
            functools.partial(attend_kernel, chunk, per, heads),
            out_shape=jax.ShapeDtypeStruct((block, channels), low),
            in_specs=in_vmem(8),
            out_specs=in_vmem(1)[0],
            scratch_shapes=[
                pltpu.VMEM((block, channels), wide),
                pltpu.VMEM((channels, 4 * channels), low),
                pltpu.VMEM((heads, width, channels), low),
                pltpu.VMEM((heads, width, 2 * channels), low),
                pltpu.VMEM((block, channels), wide),
                pltpu.VMEM((8, channels), wide),
            ],
            compiler_params=params,
            cost_estimate=pl.CostEstimate(
                flops=per * heads * width * width * channels * 6,
                bytes_accessed=2 * heads * width * width,
                transcendentals=per * heads * width * width,
            ),
            name="attend",
        )(
            moved[chunk],
            turned,
            pair_mask,
            query_weight,
            key_weight,
            value_weight,
            gate_weight,
            gate_offset.reshape(1, channels),
        )
        returned.append(
            lax.all_to_all(
                gated.reshape(groups, rows * per, channels), "dap", split_axis=0, concat_axis=0, tiled=True
            ).reshape(block, channels)
        )
    update = pl.pallas_call(
        functools.partial(finish_kernel, rows, width, groups, CHUNKS),
        out_shape=jax.ShapeDtypeStruct((rows * width, channels), low),
        in_specs=in_vmem(CHUNKS + 2),
        out_specs=in_vmem(1)[0],
        scratch_shapes=[pltpu.VMEM((block, channels), wide)] * CHUNKS + [pltpu.VMEM((2, width, channels), wide)],
        compiler_params=params,
        name="finish",
    )(*returned, out_weight, out_offset.reshape(1, channels))
    return update.reshape(rows, width, channels)


def solution(mesh):
    in_specs = (P(("dp", "dap"), None, None), P("dp", "dap")) + (P(),) * 10
    out_specs = P(("dp", "dap"), None, None)
    return jax.shard_map(local, mesh=mesh, in_specs=in_specs, out_specs=out_specs, check_vma=False)
```

time: 410 us -> 325 us (0.79)
  Pallas kernels: 0 us -> 177 us
  local copies, waits for them, and re-layouts: 127 us -> 3.36 us
  matrix products: 122 us -> 0 us
  other arithmetic: 38.9 us -> 0 us
  waiting for transfers between devices: 42.5 us -> 56.7 us
  blocking collectives: 50.3 us -> 63.6 us
    pallas_call x0 -> x5, Pallas kernels: none -> 177 us  [the longest x2 157 us: local(): pl.pallas_call(functools.partial(attend_kernel, chunk, per, heads), out_s...]
    dot_general x30 -> x0, matrix products: 122 us -> none  [the longest x12 69.1 us: per_column(): jnp.einsum('ihd,khd->hki', query_one, key_one, preferred_element_type=jnp...]
    all_gather x1, waiting for transfers between devices: 0.01 us -> 56.7 us  [local(): gathered = lax.all_gather(bias_local, 'dap', axis=0, tiled=True)]
    while x4 -> x0, local copies, waits for them, and re-layouts: 49.5 us -> none  [local(): lax.map(per_column, (query_cols, key_cols, value_cols, mask_cols))]
    all_to_all x1 -> x2, waiting for transfers between devices: 42.5 us -> 0.01 us  [the longest x1 0.01 us: local(): lax.all_to_all(send.reshape(groups, rows * per, channels), 'dap', split_a...]
    another operation x3 -> x0, local copies, waits for them, and re-layouts: 39 us -> none  [the longest x1 13 us: local(): key_cols = jnp.transpose(keys_all.reshape(heads_shape), (1, 0, 2, 3))]
    reduce_sum x14 -> x0, other arithmetic: 21.7 us -> none  [the longest x12 15.1 us: per_column(): totals = jnp.sum(probs, axis=1)]
    convert_element_type x3 -> x0, local copies, waits for them, and re-layouts: 16.8 us -> none  [local(): gated = (attended * gate.astype(jnp.float32)).astype(jnp.bfloat16)]
  transfers between devices with their start and end apart: 2 -> 3, of which waited for: 1 -> 1; matrix products, arithmetic and copies ran while one was open for 28% -> 0% of each run, Pallas kernels for 0% -> 50%
where the time goes in v1:
time: 325 us
  Pallas kernels  177 us (54%)
  blocking collectives  63.6 us (20%)
  waiting for transfers between devices  56.7 us (17%)
  between operations  13.4 us (4%)
  starting transfers between devices  10.4 us (3%)
  local copies, waits for them, and re-layouts  3.36 us (1%)
    pallas_call x2, Pallas kernels, local(): pl.pallas_call(functools.partial(attend_kernel, chunk, per, heads), out_s...  157 us
    all_gather x1, waiting for transfers between devices, local(): gathered = lax.all_gather(bias_local, 'dap', axis=0, tiled=True)  56.7 us
    all_to_all x1, blocking collectives, local(): lax.all_to_all(send.reshape(groups, rows * per, channels), 'dap', split_a...  33 us
    all_to_all x1, blocking collectives, local(): lax.all_to_all(gated.reshape(groups, rows * per, channels), 'dap', split_...  30.6 us
    pallas_call x1, Pallas kernels, local(): pl.pallas_call(functools.partial(prepare_kernel, rows, width, groups, CHU...  9.23 us
    pallas_call x1, Pallas kernels, local(): pl.pallas_call(functools.partial(turn_kernel, heads), out_shape=jax.Shape...  6.57 us
  transfers between devices with their start and end apart: 3, of which 1 were waited for; matrix products, arithmetic and copies ran while one was open for 0% of the time, Pallas kernels for 50%

profile of v1, /device:TPU:1, one launch (start us, length us, event | category | flops | bytes accessed | tf_op | source)
XLA Modules:
  0.0 324.7 jit_solution(1547807007117362217)
XLA Ops:
  6.5 0.0 all-gather.2.cloned.1.call-start
  6.5 1.4 copy.13.bias_weight_ref
  7.9 9.2 %prepare.1 = (bf16[4608,128]{1,0:T(8,128)(2,1)}, bf16[4608,128]{1,0:T(8,128)(2,1)}, bf16[48,768]{1,0:T(8,128)(2,1)}) custom-call(bf16[9216,128]{1,0:T(8,128)(2,1)} %bitcast.16, f32[1,128]{1,0:T(1,128)} %bitcast.22, f32[1,128]{1,0:T(1,128)} %bitcast.23, bf16[128,4]{1,0:T(8,128)(2,1)} %copy.13.bias_weight_ref), custom_call_target="tpu_custom_call" | custom-call | tf_op jit(solution)/shard_map/prepare/pallas_call | solution.py:204
  17.2 0.0 all-gather.2.cloned.1.call-update
  17.2 33.0 %all_to_all.20 = bf16[64,72,128]{2,1,0:T(8,128)(2,1)} all-to-all(bf16[64,72,128]{2,1,0:T(8,128)(2,1)} %bitcast.20), channel_id=1, replica_groups=mesh['dap'=64,'dp'=2] {'dap'}, dimensions={0} | all-to-all | bytes 2359296 | tf_op jit(solution)/shard_map/all_to_all | solution.py:218
  50.2 0.0 copy-start.2
  50.2 5.4 %all-to-all-start = ((bf16[64,72,128]{2,1,0:T(8,128)(2,1)}), bf16[64,72,128]{2,1,0:T(8,128)(2,1)S(1)}, u32[]{:S(2)}, u32[]{:S(2)}) async-start(bf16[64,72,128]{2,1,0:T(8,128)(2,1)} %bitcast.3), calls=%async_computation | async-start | bytes 2359296 | tf_op jit(solution)/shard_map/all_to_all | solution.py:218
  55.6 0.0 copy-done.2
  55.6 0.9 copy.14.mask_ref
  56.5 56.7 %all-gather.2.cloned.1.call-done.gathered_ref = bf16[3072,768]{1,0:T(8,128)(2,1)} async-done(((bf16[48,768]{1,0:T(8,128)(2,1)}), bf16[3072,768]{1,0:T(8,128)(2,1)}) %all-gather.2.cloned.1.call-update) | async-done | bytes 4718608 | tf_op jit(solution)/shard_map/all_gather | solution.py:216
  113.2 6.6 %turn.1.bias_ref = bf16[4,768,768]{2,1,0:T(8,128)(2,1)} custom-call(bf16[3072,768]{1,0:T(8,128)(2,1)} %all-gather.2.cloned.1.call-done.gathered_ref), custom_call_target="tpu_custom_call" | custom-call | tf_op jit(solution)/shard_map/turn/pallas_call | solution.py:223
  119.8 78.3 %attend.3 = bf16[4608,128]{1,0:T(8,128)(2,1)} custom-call(bf16[4608,128]{1,0:T(8,128)(2,1)} %bitcast.18, bf16[4,768,768]{2,1,0:T(8,128)(2,1)} %turn.1.bias_ref, s32[768,12]{1,0:T(8,128)} %copy.14.mask_ref, bf16[128,128]{1,0:T(8,128)(2,1)} %query_weight_ref.3, bf16[128,128]{1,0:T(8,128)(2,1)} %key_weight_ref.3, bf16[128,128]{1,0:T(8,128)(2,1)} %value_weight_ref.3, ...), custom_call_target="tpu_custom_call" | custom-call | flops 10871635968 | bytes 4718592 | tf_op jit(solution)/shard_map/attend/pallas_call | solution.py:235
  198.1 0.0 all-to-all-done
  198.1 0.0 copy-start.1
  198.1 1.0 copy-done.1
  199.1 5.0 %all-to-all-start.3 = ((bf16[64,72,128]{2,1,0:T(8,128)(2,1)}), bf16[64,72,128]{2,1,0:T(8,128)(2,1)S(1)}, u32[]{:S(2)}, u32[]{:S(2)}) async-start(bf16[64,72,128]{2,1,0:T(8,128)(2,1)} %bitcast.19), calls=%async_computation.3 | async-start | bytes 2359296 | tf_op jit(solution)/shard_map/all_to_all | solution.py:266
  204.2 78.3 %attend.2 = bf16[4608,128]{1,0:T(8,128)(2,1)} custom-call(bf16[4608,128]{1,0:T(8,128)(2,1)} %bitcast.17, bf16[4,768,768]{2,1,0:T(8,128)(2,1)} %turn.1.bias_ref, s32[768,12]{1,0:T(8,128)} %copy.14.mask_ref, bf16[128,128]{1,0:T(8,128)(2,1)} %query_weight_ref.3, bf16[128,128]{1,0:T(8,128)(2,1)} %key_weight_ref.3, bf16[128,128]{1,0:T(8,128)(2,1)} %value_weight_ref.3, ...), custom_call_target="tpu_custom_call" | custom-call | flops 10871635968 | bytes 4718592 | tf_op jit(solution)/shard_map/attend/pallas_call | solution.py:235
  282.5 0.0 all-to-all-done.3
  282.5 0.0 copy-start
  282.5 30.6 %all_to_all.21 = bf16[64,72,128]{2,1,0:T(8,128)(2,1)} all-to-all(bf16[64,72,128]{2,1,0:T(8,128)(2,1)} %bitcast.21), channel_id=1, replica_groups=mesh['dap'=64,'dp'=2] {'dap'}, dimensions={0} | all-to-all | bytes 2359296 | tf_op jit(solution)/shard_map/all_to_all | solution.py:266
  313.1 0.0 copy-done
  313.1 4.8 %finish.1 = bf16[9216,128]{1,0:T(8,128)(2,1)} custom-call(bf16[4608,128]{1,0:T(8,128)(2,1)} %bitcast.15, bf16[4608,128]{1,0:T(8,128)(2,1)} %bitcast.14, bf16[128,128]{1,0:T(8,128)(2,1)} %refs_2_.1, f32[1,128]{1,0:T(1,128)} %bitcast.24), custom_call_target="tpu_custom_call" | custom-call | tf_op jit(solution)/shard_map/finish/pallas_call | solution.py:270
Async XLA Ops:
  6.5 106.7 %all-gather.2.cloned.1.call-start = ((), (), s32[]{:S(2)}) async-start(), calls=%async_computation.4 | async-start | bytes 4792320 | tf_op jit(solution)/shard_map/all_gather | solution.py:216
  50.2 5.4 %copy-start.2 = (s32[768,12]{0,1:T(8,128)S(1)}, s32[768,12]{0,1:T(8,128)}, u32[]{:S(2)}) copy-start(s32[768,12]{0,1:T(8,128)} %param.13) | copy-start | bytes 110596
  50.2 147.9 %all-to-all-start = ((bf16[64,72,128]{2,1,0:T(8,128)(2,1)}), bf16[64,72,128]{2,1,0:T(8,128)(2,1)S(1)}, u32[]{:S(2)}, u32[]{:S(2)}) async-start(bf16[64,72,128]{2,1,0:T(8,128)(2,1)} %bitcast.3), calls=%async_computation | async-start | bytes 2359296 | tf_op jit(solution)/shard_map/all_to_all | solution.py:218
  198.1 1.0 copy-start.1
  199.1 83.4 %all-to-all-start.3 = ((bf16[64,72,128]{2,1,0:T(8,128)(2,1)}), bf16[64,72,128]{2,1,0:T(8,128)(2,1)S(1)}, u32[]{:S(2)}, u32[]{:S(2)}) async-start(bf16[64,72,128]{2,1,0:T(8,128)(2,1)} %bitcast.19), calls=%async_computation.3 | async-start | bytes 2359296 | tf_op jit(solution)/shard_map/all_to_all | solution.py:266
  282.5 30.6 %copy-start = (bf16[64,72,128]{2,1,0:T(8,128)(2,1)}, bf16[64,72,128]{2,1,0:T(8,128)(2,1)S(1)}, u32[]{:S(2)}) copy-start(bf16[64,72,128]{2,1,0:T(8,128)(2,1)S(1)} %all-to-all-done.3) | copy-start | bytes 3538948
Sparse Core Ops, SparseCore 0:
  17.3 95.8 all-gather.1

commit v2 on v1

v2 whole, which is shorter than its diff:
```python
import functools

import jax
import jax.numpy as jnp
from jax import lax
from jax.experimental import pallas as pl
from jax.experimental.pallas import tpu as pltpu
from jax.sharding import PartitionSpec as P

NEG_BIG = 1000000000.0
EPSILON = 1e-05
CHUNKS = 2
TOTAL_LOW = 1e-20
TOTAL_HIGH = 1e30
NT = (((1,), (1,)), ((), ()))
PLACE = ("z", "y", "x", "core")
PLACE_SIZES = (2, 4, 4, 2)
TOTAL = 64
FIRST = 8
SHIFTS = (0, 1, 2, 3)


def dot(lhs, rhs):
    return jnp.dot(lhs, rhs, preferred_element_type=jnp.float32)


def dot_nt(lhs, rhs):
    return lax.dot_general(lhs, rhs, NT, preferred_element_type=jnp.float32)


def in_vmem(count):
    return [pl.BlockSpec(memory_space=pltpu.VMEM)] * count


def norm_kernel(rows, width, heads, pair_ref, gain_ref, offset_ref, bias_weight_ref, normed_ref, bias_ref, wide_ref):
    weight = bias_weight_ref[...]
    blank = jnp.zeros_like(weight)
    both = jnp.concatenate(
        [jnp.concatenate([weight, blank], axis=1), jnp.concatenate([blank, weight], axis=1)], axis=0
    )
    for row in range(rows):
        wide = pair_ref[pl.ds(row * width, width), :].astype(jnp.float32)
        centred = wide - jnp.mean(wide, axis=1, keepdims=True)
        spread = jnp.mean(centred * centred, axis=1, keepdims=True)
        normed = centred * lax.rsqrt(spread + EPSILON) * gain_ref[...] + offset_ref[...]
        normed_ref[pl.ds(row * width, width), :] = normed.astype(jnp.bfloat16)
        if row % 2:
            two = [normed_ref[pl.ds(at * width, width), :] for at in (row - 1, row)]
            wide_ref[pl.ds((row - 1) * heads, 2 * heads), :] = dot_nt(both, jnp.concatenate(two, axis=1))
    for copy in range(bias_ref.shape[0] // (rows * heads)):
        bias_ref[pl.ds(copy * rows * heads, rows * heads), :] = wide_ref[...].astype(jnp.bfloat16)


def layout_kernel(rows, width, groups, chunks, normed_ref, *refs):
    chunk_refs, wide_ref, staged_refs = refs[:chunks], refs[chunks], refs[chunks + 1 :]
    cols = width // groups
    per = cols // chunks
    for row in range(rows):
        wide_ref[row % 2] = normed_ref[pl.ds(row * width, width), :].astype(jnp.float32)
        for col in range(cols):
            chunk, place = divmod(col, per)
            staged_refs[chunk][pl.ds(row * per + place, groups, stride=rows * per), :] = wide_ref[
                row % 2, pl.ds(col, groups, stride=cols), :
            ]
    for chunk in range(chunks):
        chunk_refs[chunk][...] = staged_refs[chunk][...].astype(jnp.bfloat16)


def hold_kernel(*refs):
    pass


def hold(*arrays):
    whole = [pl.BlockSpec(memory_space=pl.ANY)] * len(arrays)
    return pl.pallas_call(
        hold_kernel,
        out_shape=[jax.ShapeDtypeStruct(one.shape, one.dtype) for one in arrays],
        in_specs=whole,
        out_specs=whole,
        input_output_aliases={at: at for at in range(len(arrays))},
        name="hold",
    )(*arrays)


def place_of(index):
    place = {}
    for axis, size in zip(reversed(PLACE), reversed(PLACE_SIZES)):
        place[axis] = index % size if isinstance(index, int) else lax.rem(index, size)
        index = index // size
    return place


def index_of(place):
    index = 0
    for axis, size in zip(PLACE, PLACE_SIZES):
        index = index * size + place[axis]
    return index


ORDER = (("y", "x"), ("x", "y"))


def first_groups():
    groups = {}
    for index in range(TOTAL):
        place = place_of(index)
        groups.setdefault((place["core"], place[ORDER[place["core"]][1]]), []).append(index)
    return list(groups.values())


def second_pairs(step):
    pairs = []
    for index in range(TOTAL):
        place = place_of(index)
        axis = ORDER[place["core"]][1]
        pairs.append((index, index_of({**place, axis: (place[axis] + step) % 4})))
    return pairs


def gather_bias(bias_copies, sends):
    first = lax.all_to_all(
        bias_copies.reshape((FIRST, bias_copies.shape[0] // FIRST, bias_copies.shape[1])),
        "dap",
        split_axis=0,
        concat_axis=0,
        axis_index_groups=first_groups(),
        tiled=True,
    ).reshape(bias_copies.shape)
    first, *sends = hold(first, *sends)
    pieces = [first if step == 0 else lax.ppermute(first, "dap", second_pairs(step)) for step in SHIFTS]
    other_core = [(index, index ^ 1) for index in range(TOTAL)]
    return pieces + [lax.ppermute(piece, "dap", other_core) for piece in pieces], sends


def turn_kernel(heads, rows, handed, *refs):
    count = 2 * len(SHIFTS)
    pieces, turned_ref, wide_ref = refs[:count], refs[count + handed], refs[-1]
    width = turned_ref.shape[1]
    tile = wide_ref.shape[2]
    here = place_of(lax.axis_index("dap"))
    block = rows * heads

    def unpack(core, my_pieces):
        first, second = ORDER[core]
        for far, step in enumerate(SHIFTS):
            for place in range(FIRST):
                at = {
                    "z": place // 4,
                    "core": core,
                    first: place % 4,
                    second: lax.rem(here[second] + 4 - step, 4),
                }
                start = pl.multiple_of(index_of(at) * block, 16)
                for lane in range(width // tile):
                    wide_ref[lane, pl.ds(start, block), :] = my_pieces[far][
                        pl.ds(place * block, block), lane * tile : (lane + 1) * tile
                    ].astype(jnp.float32)

    for core in range(2):

        @pl.when(here["core"] == core)
        def _():
            unpack(core, pieces[: len(SHIFTS)])
            unpack(1 - core, pieces[len(SHIFTS) :])

    unit = (
        lax.broadcasted_iota(jnp.int32, (tile, tile), 0) == lax.broadcasted_iota(jnp.int32, (tile, tile), 1)
    ).astype(jnp.bfloat16)
    for head in range(heads):
        for at in range(0, width, tile):
            one = wide_ref[at // tile, pl.ds(head, width, stride=heads), :].astype(jnp.bfloat16)
            turned_ref[head, pl.ds(at, tile), :] = dot_nt(unit, one).astype(jnp.bfloat16)


def attend_kernel(
    chunk,
    per,
    heads,
    moved_ref,
    bias_ref,
    mask_ref,
    query_weight_ref,
    key_weight_ref,
    value_weight_ref,
    gate_weight_ref,
    gate_offset_ref,
    out_ref,
    source_ref,
    weight_ref,
    present_ref,
    result_ref,
    fine_ref,
    *sets,
):
    channels = moved_ref.shape[1]
    width, mask_cols = mask_ref.shape
    head_dim = channels // heads
    source_ref[...] = moved_ref[...].astype(jnp.float32)
    for at, ref in enumerate((query_weight_ref, key_weight_ref, value_weight_ref, gate_weight_ref)):
        weight_ref[:, at * channels : (at + 1) * channels] = ref[...]
    present_ref[...] = mask_ref[...].astype(jnp.float32).astype(jnp.bfloat16)
    lane_head = lax.broadcasted_iota(jnp.int32, (1, channels), 1) // head_dim
    own = [(lane_head == head).astype(jnp.bfloat16) for head in range(heads)]
    fine_ref[...] = jnp.ones_like(fine_ref)
    share = width // heads
    first_set, second_set = sets[:5], sets[5:]

    def project(col, part, buffers, hide=True):
        query_ref, key_ref, value_ref, gate_ref, _ = buffers
        rows = pl.ds(part * share, share)
        source = source_ref[pl.ds(col + part * share * per, share, stride=per), :].astype(jnp.bfloat16)
        wide = dot(source, weight_ref[...])
        query_ref[rows, :] = (wide[:, :channels] * head_dim ** (-0.5)).astype(jnp.bfloat16)
        key_ref[rows, :] = wide[:, channels : 2 * channels].astype(jnp.bfloat16)
        pick = (lax.broadcasted_iota(jnp.int32, (mask_cols, channels), 0) == chunk * per + col).astype(jnp.bfloat16)
        present = dot(present_ref[rows, :], pick).astype(jnp.bfloat16)
        values = wide[:, 2 * channels : 3 * channels].astype(jnp.bfloat16)
        value_ref[rows, :channels] = values * present if hide else values
        value_ref[rows, channels:] = present
        gate_ref[rows, :] = jax.nn.sigmoid(wide[:, 3 * channels :] + gate_offset_ref[...]).astype(jnp.bfloat16)

    def attend(head, buffers):
        query_ref, key_ref, value_ref, _, total_ref = buffers
        scores = dot_nt(query_ref[...] * own[head], key_ref[...]) + bias_ref[head].astype(jnp.float32)
        total = dot(jnp.exp(scores).astype(jnp.bfloat16), value_ref[...])
        for low in (head * head_dim, channels + head * head_dim):
            total_ref[:, low : low + head_dim] = total[:, low : low + head_dim]

    def close(col, buffers):
        _, _, _, gate_ref, total_ref = buffers
        sums = total_ref[:, channels:]
        fine = jnp.where((sums > TOTAL_LOW) & (sums < TOTAL_HIGH), 1.0, 0.0)
        fine_ref[...] = jnp.minimum(fine_ref[...], jnp.min(fine.reshape(width // 8, 8, channels), axis=0))
        result_ref[pl.ds(col, width, stride=per), :] = (
            total_ref[:, :channels] / sums * gate_ref[...].astype(jnp.float32)
        )

    for part in range(heads):
        project(0, part, first_set)

    def two_columns(step, carry):
        for now, later, col in ((first_set, second_set, 2 * step), (second_set, first_set, 2 * step + 1)):
            for head in range(heads):
                attend(head, now)
                project(jnp.minimum(col + 1, per - 1), head, later)
            close(col, now)
        return carry

    lax.fori_loop(0, per // 2, two_columns, 0)

    @pl.when(jnp.min(fine_ref[...]) < 0.5)
    def _():
        tile = 128
        query_ref, key_ref, value_ref, gate_ref, total_ref = first_set

        def exact(col, carry):
            for part in range(heads):
                project(col, part, first_set, hide=False)
            first = (lax.broadcasted_iota(jnp.int32, (8, channels), 1) == 0).astype(jnp.bfloat16)
            lift = NEG_BIG * (dot_nt(first, value_ref[:, channels:])[:1] - 1.0)

            def rows_exact(step, inner):
                rows = pl.ds(pl.multiple_of(step * tile, tile), tile)
                for head in range(heads):
                    low = head * head_dim
                    scores = dot_nt(query_ref[rows, :] * own[head], key_ref[...])
                    scores = scores + bias_ref[head, rows, :].astype(jnp.float32) + lift
                    probs = jnp.exp(scores - jnp.max(scores, axis=1, keepdims=True))
                    totals = jnp.sum(probs, axis=1, keepdims=True)
                    attended = dot(probs.astype(jnp.bfloat16), value_ref[:, :channels]) / totals
                    total_ref[rows, low : low + head_dim] = attended[:, low : low + head_dim]
                return inner

            lax.fori_loop(0, width // tile, rows_exact, 0)
            result_ref[pl.ds(col, width, stride=per), :] = total_ref[:, :channels] * gate_ref[...].astype(jnp.float32)
            return carry

        lax.fori_loop(0, per, exact, 0)

    out_ref[...] = result_ref[...].astype(jnp.bfloat16)


def finish_kernel(rows, width, groups, chunks, *refs):
    chunk_refs = refs[:chunks]
    out_weight_ref, out_offset_ref, update_ref = refs[chunks : chunks + 3]
    wide_refs = refs[chunks + 3 : 2 * chunks + 3]
    row_ref = refs[2 * chunks + 3]
    cols = width // groups
    per = cols // chunks
    for chunk in range(chunks):
        wide_refs[chunk][...] = dot(chunk_refs[chunk][...], out_weight_ref[...]) + out_offset_ref[...]
    for row in range(rows):
        for col in range(cols):
            chunk, place = divmod(col, per)
            row_ref[row % 2, pl.ds(col, groups, stride=cols), :] = wide_refs[chunk][
                pl.ds(row * per + place, groups, stride=rows * per), :
            ]
        update_ref[pl.ds(row * width, width), :] = row_ref[row % 2].astype(jnp.bfloat16)


def local(
    pair,
    pair_mask,
    ln_gain,
    ln_offset,
    bias_weight,
    query_weight,
    key_weight,
    value_weight,
    gate_weight,
    gate_offset,
    out_weight,
    out_offset,
):
    rows, width, channels = pair.shape
    groups = lax.axis_size("dap")
    cols = width // groups
    per = cols // CHUNKS
    heads = bias_weight.shape[1]
    block = groups * rows * per
    low, wide = jnp.bfloat16, jnp.float32
    params = pltpu.CompilerParams(vmem_limit_bytes=56 * 1024 * 1024)
    normed, bias_copies = pl.pallas_call(
        functools.partial(norm_kernel, rows, width, heads),
        out_shape=[
            jax.ShapeDtypeStruct((rows * width, channels), low),
            jax.ShapeDtypeStruct((FIRST * rows * heads, width), low),
        ],
        in_specs=in_vmem(4),
        out_specs=in_vmem(2),
        scratch_shapes=[pltpu.VMEM((rows * heads, width), wide)],
        compiler_params=params,
        name="norm",
    )(pair.reshape(rows * width, channels), ln_gain.reshape(1, channels), ln_offset.reshape(1, channels), bias_weight.T)
    sends = pl.pallas_call(
        functools.partial(layout_kernel, rows, width, groups, CHUNKS),
        out_shape=[jax.ShapeDtypeStruct((block, channels), low)] * CHUNKS,
        in_specs=in_vmem(1),
        out_specs=in_vmem(CHUNKS),
        scratch_shapes=[pltpu.VMEM((2, width, channels), wide)] + [pltpu.VMEM((block, channels), wide)] * CHUNKS,
        compiler_params=params,
        cost_estimate=pl.CostEstimate(flops=10**6, bytes_accessed=15 * 10**6, transcendentals=0),
        name="layout",
    )(normed)

    pieces, sends = gather_bias(bias_copies, sends)
    whole = pl.BlockSpec(memory_space=pl.ANY)
    later = sends[1:]
    turned, *later = pl.pallas_call(
        functools.partial(turn_kernel, heads, rows, len(later)),
        out_shape=[jax.ShapeDtypeStruct((heads, width, width), low)]
        + [jax.ShapeDtypeStruct(one.shape, one.dtype) for one in later],
        in_specs=in_vmem(len(pieces)) + [whole] * len(later),
        out_specs=in_vmem(1) + [whole] * len(later),
        input_output_aliases={len(pieces) + at: 1 + at for at in range(len(later))},
        scratch_shapes=[pltpu.VMEM((width // channels, width * heads, channels), wide)],
        compiler_params=params,
        name="turn",
    )(*pieces, *later)
    moved = [
        lax.all_to_all(
            send.reshape(groups, rows * per, channels), "dap", split_axis=0, concat_axis=0, tiled=True
        ).reshape(block, channels)
        for send in (sends[0], *later)
    ]

    returned = []
    for chunk in range(CHUNKS):
        gated = pl.pallas_call(
            functools.partial(attend_kernel, chunk, per, heads),
            out_shape=jax.ShapeDtypeStruct((block, channels), low),
            in_specs=in_vmem(8),
            out_specs=in_vmem(1)[0],
            scratch_shapes=[
                pltpu.VMEM((block, channels), wide),
                pltpu.VMEM((channels, 4 * channels), low),
                pltpu.VMEM(pair_mask.shape, low),
                pltpu.VMEM((block, channels), wide),
                pltpu.VMEM((8, channels), wide),
            ]
            + 2
            * [
                pltpu.VMEM((width, channels), low),
                pltpu.VMEM((width, channels), low),
                pltpu.VMEM((width, 2 * channels), low),
                pltpu.VMEM((width, channels), low),
                pltpu.VMEM((width, 2 * channels), wide),
            ],
            compiler_params=params,
            cost_estimate=pl.CostEstimate(
                flops=per * heads * width * width * channels * 6,
                bytes_accessed=2 * heads * width * width,
                transcendentals=per * heads * width * width,
            ),
            name="attend",
        )(
            moved[chunk],
            turned,
            pair_mask,
            query_weight,
            key_weight,
            value_weight,
            gate_weight,
            gate_offset.reshape(1, channels),
        )
        returned.append(
            lax.all_to_all(
                gated.reshape(groups, rows * per, channels), "dap", split_axis=0, concat_axis=0, tiled=True
            ).reshape(block, channels)
        )
    update = pl.pallas_call(
        functools.partial(finish_kernel, rows, width, groups, CHUNKS),
        out_shape=jax.ShapeDtypeStruct((rows * width, channels), low),
        in_specs=in_vmem(CHUNKS + 2),
        out_specs=in_vmem(1)[0],
        scratch_shapes=[pltpu.VMEM((block, channels), wide)] * CHUNKS + [pltpu.VMEM((2, width, channels), wide)],
        compiler_params=params,
        name="finish",
    )(*returned, out_weight, out_offset.reshape(1, channels))
    return update.reshape(rows, width, channels)


def solution(mesh):
    in_specs = (P(("dp", "dap"), None, None), P("dp", "dap")) + (P(),) * 10
    out_specs = P(("dp", "dap"), None, None)
    return jax.shard_map(local, mesh=mesh, in_specs=in_specs, out_specs=out_specs, check_vma=False)
```

time: 325 us -> 273 us (0.84)
  waiting for transfers between devices: 56.7 us -> 14.2 us
  starting transfers between devices: 10.4 us -> 45.1 us
  blocking collectives: 63.6 us -> 30.6 us
  between operations: 13.4 us -> 0.12 us
    all_gather x1 -> x0, waiting for transfers between devices: 56.7 us -> none  [local(): gathered = lax.all_gather(bias_local, 'dap', axis=0, tiled=True)]
    all_to_all x1 -> x0, blocking collectives: 33 us -> none  [local(): lax.all_to_all(send.reshape(groups, rows * per, channels), 'dap', split_a...]
    ppermute x0 -> x7, starting transfers between devices: none -> 11.4 us  [the longest x4 6.3 us: gather_bias(): lax.ppermute(piece, 'dap', other_core)]
    all_to_all x1 -> x2, starting transfers between devices: 5.38 us -> 15.1 us  [local(): lax.all_to_all(send.reshape(groups, rows * per, channels), 'dap', split_a...]
    ppermute x0 -> x7, waiting for transfers between devices: none -> 8.54 us  [the longest x3 6.95 us: gather_bias(): lax.ppermute(first, 'dap', second_pairs(step))]
    all_to_all x0 -> x1, starting transfers between devices: none -> 8.16 us  [gather_bias(): lax.all_to_all(bias_copies.reshape((FIRST, bias_copies.shape[0] // FIRST,...]
    all_to_all x0 -> x1, waiting for transfers between devices: none -> 5.68 us  [gather_bias(): lax.all_to_all(bias_copies.reshape((FIRST, bias_copies.shape[0] // FIRST,...]
    all_to_all x1, starting transfers between devices: 5.03 us -> 10.4 us  [local(): lax.all_to_all(gated.reshape(groups, rows * per, channels), 'dap', split_...]
  transfers between devices with their start and end apart: 3 -> 11, of which waited for: 1 -> 3; matrix products, arithmetic and copies ran while one was open for 0% -> 0% of each run, Pallas kernels for 50% -> 61%
where the time goes in v2:
time: 273 us; the launch traced here: 272 us
  Pallas kernels  178 us (65%)
  starting transfers between devices  45.1 us (17%)
  blocking collectives  30.6 us (11%)
  waiting for transfers between devices  14.2 us (5%)
  local copies, waits for them, and re-layouts  4.61 us (2%)
    pallas_call x2, Pallas kernels, local(): pl.pallas_call(functools.partial(attend_kernel, chunk, per, heads), out_s...  156 us
    all_to_all x1, blocking collectives, local(): lax.all_to_all(gated.reshape(groups, rows * per, channels), 'dap', split_...  30.6 us
    all_to_all x2, starting transfers between devices, local(): lax.all_to_all(send.reshape(groups, rows * per, channels), 'dap', split_a...  15.1 us
    all_to_all x1, starting transfers between devices, local(): lax.all_to_all(gated.reshape(groups, rows * per, channels), 'dap', split_...  10.4 us
    all_to_all x1, starting transfers between devices, gather_bias(): lax.all_to_all(bias_copies.reshape((FIRST, bias_copies.shape[0] // FIRST,...  8.16 us
    ppermute x3, waiting for transfers between devices, gather_bias(): lax.ppermute(first, 'dap', second_pairs(step))  6.95 us
    pallas_call x1, Pallas kernels, local(): pl.pallas_call(functools.partial(turn_kernel, heads, rows, len(later)), o...  6.48 us
    ppermute x4, starting transfers between devices, gather_bias(): lax.ppermute(piece, 'dap', other_core)  6.3 us
  transfers between devices with their start and end apart: 11, of which 3 were waited for; matrix products, arithmetic and copies ran while one was open for 0% of the time, Pallas kernels for 61%

profile of v2, /device:TPU:1, one launch (start us, length us, event | category | flops | bytes accessed | tf_op | source)
XLA Modules:
  0.0 272.3 jit_solution(8691839077927285950)
XLA Ops:
  0.0 6.0 %norm.1 = (bf16[9216,128]{1,0:T(8,128)(2,1)}, bf16[384,768]{1,0:T(8,128)(2,1)}) custom-call(bf16[9216,128]{1,0:T(8,128)(2,1)} %bitcast.22, f32[1,128]{1,0:T(1,128)} %bitcast.30, f32[1,128]{1,0:T(1,128)} %bitcast.31, bf16[4,128]{1,0:T(4,128)(2,1)} %bitcast.28), custom_call_target="tpu_custom_call" | custom-call | tf_op jit(solution)/shard_map/norm/pallas_call | solution.py:323
  6.0 8.2 %all-to-all-start = ((bf16[8,48,768]{2,1,0:T(8,128)(2,1)}), bf16[8,48,768]{2,1,0:T(8,128)(2,1)S(1)}, u32[]{:S(2)}, u32[]{:S(2)}) async-start(bf16[8,48,768]{2,1,0:T(8,128)(2,1)} %bitcast.27), calls=%async_computation | async-start | bytes 1179648 | tf_op jit(solution)/shard_map/all_to_all | solution.py:121
  14.1 4.5 %layout.1 = (bf16[4608,128]{1,0:T(8,128)(2,1)}, bf16[4608,128]{1,0:T(8,128)(2,1)}) custom-call(bf16[9216,128]{1,0:T(8,128)(2,1)} %get-tuple-element.15.normed_ref), custom_call_target="tpu_custom_call" | custom-call | flops 1000000 | bytes 15000000 | tf_op jit(solution)/shard_map/layout/pallas_call | solution.py:335
  18.6 5.7 %all-to-all-done = bf16[8,48,768]{2,1,0:T(8,128)(2,1)S(1)} async-done(((bf16[8,48,768]{2,1,0:T(8,128)(2,1)}), bf16[8,48,768]{2,1,0:T(8,128)(2,1)S(1)}, u32[]{:S(2)}, u32[]{:S(2)}) %all-to-all-start) | async-done | bytes 589856 | tf_op jit(solution)/shard_map/all_to_all | solution.py:121
  24.3 0.0 copy-start
  24.3 0.8 copy-done
  25.1 1.5 collective-permute-start
  26.6 2.7 %collective-permute-start.1 = (bf16[384,768]{1,0:T(8,128)(2,1)}, bf16[384,768]{1,0:T(8,128)(2,1)S(1)}, u32[]{:S(2)}, u32[]{:S(2)}) collective-permute-start(bf16[384,768]{1,0:T(8,128)(2,1)} %get-tuple-element.19.refs_0_), channel_id=1, source_target_pairs={{0,8},{2,34},{4,12},{6,38},{8,0},{10,42},{12,4},{14,46},{16,24},{1... | collective-permute-start | bytes 1769480 | tf_op jit(solution)/shard_map/ppermute | solution.py:130
  29.3 0.9 collective-permute-start.2
  30.3 0.0 copy-start.1
  30.3 7.1 %all-to-all-start.1 = ((bf16[64,72,128]{2,1,0:T(8,128)(2,1)}), bf16[64,72,128]{2,1,0:T(8,128)(2,1)S(1)}, u32[]{:S(2)}, u32[]{:S(2)}) async-start(bf16[64,72,128]{2,1,0:T(8,128)(2,1)} %bitcast.21), calls=%async_computation.1 | async-start | bytes 2359296 | tf_op jit(solution)/shard_map/all_to_all | solution.py:361
  37.4 0.0 copy-done.1
  37.4 0.5 collective-permute-start.3
  38.0 0.0 collective-permute-done.refs_1_
  38.0 0.0 copy-start.5
  38.0 0.3 collective-permute-start.4
  38.3 6.9 %collective-permute-done.1.refs_2_ = bf16[384,768]{1,0:T(8,128)(2,1)S(1)} collective-permute-done((bf16[384,768]{1,0:T(8,128)(2,1)}, bf16[384,768]{1,0:T(8,128)(2,1)S(1)}, u32[]{:S(2)}, u32[]{:S(2)}) %collective-permute-start.1) | collective-permute-done | bytes 589856 | tf_op jit(solution)/shard_map/ppermute | solution.py:130
  45.2 0.0 copy-start.6
  45.2 3.4 %collective-permute-start.5 = (bf16[384,768]{1,0:T(8,128)(2,1)S(1)}, bf16[384,768]{1,0:T(8,128)(2,1)S(1)}, u32[]{:S(2)}, u32[]{:S(2)}) collective-permute-start(bf16[384,768]{1,0:T(8,128)(2,1)S(1)} %collective-permute-done.1.refs_2_), channel_id=1, source_target_pairs={{0,2},{2,0},{4,6},{6,4},{8,10},{10,8},{12,14},{14,12},{16,18},{18,... | collective-permute-start | bytes 1769480 | tf_op jit(solution)/shard_map/ppermute | solution.py:132
  48.6 0.0 collective-permute-done.2.refs_3_
  48.6 0.0 copy-start.7
  48.6 2.1 collective-permute-start.6
  50.7 0.0 collective-permute-done.3.refs_4_
  50.7 0.0 copy-start.8
  50.7 0.0 collective-permute-done.4.refs_5_
  50.7 0.0 copy-start.9
  50.7 0.0 collective-permute-done.5.refs_6_
  50.7 0.0 copy-start.10
  50.7 1.6 collective-permute-done.6.refs_7_
  52.3 0.0 copy-start.11
  52.3 0.0 copy-done.5
  52.3 0.0 copy-done.6
  52.3 0.0 copy-done.7
  52.3 0.0 copy-done.8
  52.3 0.0 copy-done.9
  52.3 0.0 copy-done.10
  52.3 0.8 copy-done.11
  53.1 6.5 %turn.1 = (bf16[4,768,768]{2,1,0:T(8,128)(2,1)}, bf16[4608,128]{1,0:T(8,128)(2,1)}) custom-call(bf16[384,768]{1,0:T(8,128)(2,1)} %get-tuple-element.19.refs_0_, bf16[384,768]{1,0:T(8,128)(2,1)} %copy-done.5, bf16[384,768]{1,0:T(8,128)(2,1)} %copy-done.6, bf16[384,768]{1,0:T(8,128)(2,1)} %copy-done.7, ...), custom_call_target="tpu_custom_call", output_to_operand_aliasing={{1}: (8, {})} | custom-call | tf_op jit(solution)/shard_map/turn/pallas_call | solution.py:349
  59.6 0.0 all-to-all-done.1
  59.6 0.0 copy-start.3
  59.6 0.0 copy-start.12
  59.6 1.0 copy-done.3
  60.6 8.0 %all-to-all-start.3 = ((bf16[64,72,128]{2,1,0:T(8,128)(2,1)}), bf16[64,72,128]{2,1,0:T(8,128)(2,1)S(1)}, u32[]{:S(2)}, u32[]{:S(2)}) async-start(bf16[64,72,128]{2,1,0:T(8,128)(2,1)} %bitcast.17), calls=%async_computation.3 | async-start | bytes 2359296 | tf_op jit(solution)/shard_map/all_to_all | solution.py:361
  68.6 0.0 copy-done.12
  68.6 1.0 copy.17.mask_ref
  69.6 78.0 %attend.2 = bf16[4608,128]{1,0:T(8,128)(2,1)} custom-call(bf16[4608,128]{1,0:T(8,128)(2,1)} %bitcast.23, bf16[4,768,768]{2,1,0:T(8,128)(2,1)} %get-tuple-element.21.bias_ref, s32[768,12]{1,0:T(8,128)} %copy.17.mask_ref, bf16[128,128]{1,0:T(8,128)(2,1)} %query_weight_ref.3, bf16[128,128]{1,0:T(8,128)(2,1)} %key_weight_ref.3, ...), custom_call_target="tpu_custom_call" | custom-call | flops 10871635968 | bytes 4718592 | tf_op jit(solution)/shard_map/attend/pallas_call | solution.py:369
  147.5 0.0 all-to-all-done.3
  147.5 0.0 copy-start.4
  147.5 1.0 copy-done.4
  148.5 10.4 %all-to-all-start.2 = ((bf16[64,72,128]{2,1,0:T(8,128)(2,1)}), bf16[64,72,128]{2,1,0:T(8,128)(2,1)S(1)}, u32[]{:S(2)}, u32[]{:S(2)}) async-start(bf16[64,72,128]{2,1,0:T(8,128)(2,1)} %bitcast.25), calls=%async_computation.2 | async-start | bytes 2359296 | tf_op jit(solution)/shard_map/all_to_all | solution.py:407
  159.0 77.9 %attend.3 = bf16[4608,128]{1,0:T(8,128)(2,1)} custom-call(bf16[4608,128]{1,0:T(8,128)(2,1)} %bitcast.24, bf16[4,768,768]{2,1,0:T(8,128)(2,1)} %get-tuple-element.21.bias_ref, s32[768,12]{1,0:T(8,128)} %copy.17.mask_ref, bf16[128,128]{1,0:T(8,128)(2,1)} %query_weight_ref.3, bf16[128,128]{1,0:T(8,128)(2,1)} %key_weight_ref.3, ...), custom_call_target="tpu_custom_call" | custom-call | flops 10871635968 | bytes 4718592 | tf_op jit(solution)/shard_map/attend/pallas_call | solution.py:369
  236.9 0.0 all-to-all-done.2
  236.9 0.0 copy-start.2
  236.9 30.6 %all_to_all.25 = bf16[64,72,128]{2,1,0:T(8,128)(2,1)} all-to-all(bf16[64,72,128]{2,1,0:T(8,128)(2,1)} %bitcast.26), channel_id=1, replica_groups=mesh['dap'=64,'dp'=2] {'dap'}, dimensions={0} | all-to-all | bytes 2359296 | tf_op jit(solution)/shard_map/all_to_all | solution.py:407
  267.5 0.0 copy-done.2
  267.5 4.8 %finish.1 = bf16[9216,128]{1,0:T(8,128)(2,1)} custom-call(bf16[4608,128]{1,0:T(8,128)(2,1)} %bitcast.19, bf16[4608,128]{1,0:T(8,128)(2,1)} %bitcast.20, bf16[128,128]{1,0:T(8,128)(2,1)} %refs_2_.1, f32[1,128]{1,0:T(1,128)} %bitcast.29), custom_call_target="tpu_custom_call" | custom-call | tf_op jit(solution)/shard_map/finish/pallas_call | solution.py:411
  (1 shorter events, 0.0 us)
Async XLA Ops:
  6.0 18.3 %all-to-all-start = ((bf16[8,48,768]{2,1,0:T(8,128)(2,1)}), bf16[8,48,768]{2,1,0:T(8,128)(2,1)S(1)}, u32[]{:S(2)}, u32[]{:S(2)}) async-start(bf16[8,48,768]{2,1,0:T(8,128)(2,1)} %bitcast.27), calls=%async_computation | async-start | bytes 1179648 | tf_op jit(solution)/shard_map/all_to_all | solution.py:121
  24.3 0.8 copy-start
  25.1 12.8 %collective-permute-start = (bf16[384,768]{1,0:T(8,128)(2,1)}, bf16[384,768]{1,0:T(8,128)(2,1)S(1)}, u32[]{:S(2)}, u32[]{:S(2)}) collective-permute-start(bf16[384,768]{1,0:T(8,128)(2,1)} %get-tuple-element.19.refs_0_), channel_id=1, source_target_pairs={{0,4},{2,18},{4,8},{6,22},{8,12},{10,26},{12,0},{14,30},{16,20},{1... | collective-permute-start | bytes 1769480 | tf_op jit(solution)/shard_map/ppermute | solution.py:130
  26.6 18.6 %collective-permute-start.1 = (bf16[384,768]{1,0:T(8,128)(2,1)}, bf16[384,768]{1,0:T(8,128)(2,1)S(1)}, u32[]{:S(2)}, u32[]{:S(2)}) collective-permute-start(bf16[384,768]{1,0:T(8,128)(2,1)} %get-tuple-element.19.refs_0_), channel_id=1, source_target_pairs={{0,8},{2,34},{4,12},{6,38},{8,0},{10,42},{12,4},{14,46},{16,24},{1... | collective-permute-start | bytes 1769480 | tf_op jit(solution)/shard_map/ppermute | solution.py:130
  29.3 19.3 %collective-permute-start.2 = (bf16[384,768]{1,0:T(8,128)(2,1)}, bf16[384,768]{1,0:T(8,128)(2,1)S(1)}, u32[]{:S(2)}, u32[]{:S(2)}) collective-permute-start(bf16[384,768]{1,0:T(8,128)(2,1)} %get-tuple-element.19.refs_0_), channel_id=1, source_target_pairs={{0,12},{2,50},{4,0},{6,54},{8,4},{10,58},{12,8},{14,62},{16,28},{1... | collective-permute-start | bytes 1769480 | tf_op jit(solution)/shard_map/ppermute | solution.py:130
  30.3 7.2 %copy-start.1 = (bf16[384,768]{1,0:T(8,128)(2,1)S(1)}, bf16[384,768]{1,0:T(8,128)(2,1)}, u32[]{:S(2)}) copy-start(bf16[384,768]{1,0:T(8,128)(2,1)} %get-tuple-element.19.refs_0_) | copy-start | bytes 1769476
  30.3 29.4 %all-to-all-start.1 = ((bf16[64,72,128]{2,1,0:T(8,128)(2,1)}), bf16[64,72,128]{2,1,0:T(8,128)(2,1)S(1)}, u32[]{:S(2)}, u32[]{:S(2)}) async-start(bf16[64,72,128]{2,1,0:T(8,128)(2,1)} %bitcast.21), calls=%async_computation.1 | async-start | bytes 2359296 | tf_op jit(solution)/shard_map/all_to_all | solution.py:361
  37.4 13.3 %collective-permute-start.3 = (bf16[384,768]{1,0:T(8,128)(2,1)S(1)}, bf16[384,768]{1,0:T(8,128)(2,1)S(1)}, u32[]{:S(2)}, u32[]{:S(2)}) collective-permute-start(bf16[384,768]{1,0:T(8,128)(2,1)S(1)} %copy-done.1), channel_id=1, source_target_pairs={{0,2},{2,0},{4,6},{6,4},{8,10},{10,8},{12,14},{14,12},{16,18},{18,... | collective-permute-start | bytes 1769480 | tf_op jit(solution)/shard_map/ppermute | solution.py:132
  38.0 14.3 %copy-start.5 = (bf16[384,768]{1,0:T(8,128)(2,1)}, bf16[384,768]{1,0:T(8,128)(2,1)S(1)}, u32[]{:S(2)}) copy-start(bf16[384,768]{1,0:T(8,128)(2,1)S(1)} %collective-permute-done.refs_1_) | copy-start | bytes 1769476
  38.0 12.7 %collective-permute-start.4 = (bf16[384,768]{1,0:T(8,128)(2,1)S(1)}, bf16[384,768]{1,0:T(8,128)(2,1)S(1)}, u32[]{:S(2)}, u32[]{:S(2)}) collective-permute-start(bf16[384,768]{1,0:T(8,128)(2,1)S(1)} %collective-permute-done.refs_1_), channel_id=1, source_target_pairs={{0,2},{2,0},{4,6},{6,4},{8,10},{10,8},{12,14},{14,12},{16,18},{18,... | collective-permute-start | bytes 1769480 | tf_op jit(solution)/shard_map/ppermute | solution.py:132
  45.2 7.1 %copy-start.6 = (bf16[384,768]{1,0:T(8,128)(2,1)}, bf16[384,768]{1,0:T(8,128)(2,1)S(1)}, u32[]{:S(2)}) copy-start(bf16[384,768]{1,0:T(8,128)(2,1)S(1)} %collective-permute-done.1.refs_2_) | copy-start | bytes 1769476
  45.2 5.5 %collective-permute-start.5 = (bf16[384,768]{1,0:T(8,128)(2,1)S(1)}, bf16[384,768]{1,0:T(8,128)(2,1)S(1)}, u32[]{:S(2)}, u32[]{:S(2)}) collective-permute-start(bf16[384,768]{1,0:T(8,128)(2,1)S(1)} %collective-permute-done.1.refs_2_), channel_id=1, source_target_pairs={{0,2},{2,0},{4,6},{6,4},{8,10},{10,8},{12,14},{14,12},{16,18},{18,... | collective-permute-start | bytes 1769480 | tf_op jit(solution)/shard_map/ppermute | solution.py:132
  48.6 3.7 %copy-start.7 = (bf16[384,768]{1,0:T(8,128)(2,1)}, bf16[384,768]{1,0:T(8,128)(2,1)S(1)}, u32[]{:S(2)}) copy-start(bf16[384,768]{1,0:T(8,128)(2,1)S(1)} %collective-permute-done.2.refs_3_) | copy-start | bytes 1769476
  48.6 3.7 %collective-permute-start.6 = (bf16[384,768]{1,0:T(8,128)(2,1)S(1)}, bf16[384,768]{1,0:T(8,128)(2,1)S(1)}, u32[]{:S(2)}, u32[]{:S(2)}) collective-permute-start(bf16[384,768]{1,0:T(8,128)(2,1)S(1)} %collective-permute-done.2.refs_3_), channel_id=1, source_target_pairs={{0,2},{2,0},{4,6},{6,4},{8,10},{10,8},{12,14},{14,12},{16,18},{18,... | collective-permute-start | bytes 1769480 | tf_op jit(solution)/shard_map/ppermute | solution.py:132
  50.7 1.6 copy-start.8
  50.7 1.6 copy-start.9
  50.7 1.6 copy-start.10
  52.3 0.8 copy-start.11
  59.6 1.0 copy-start.3
  59.6 9.0 %copy-start.12 = (s32[768,12]{0,1:T(8,128)S(1)}, s32[768,12]{0,1:T(8,128)}, u32[]{:S(2)}) copy-start(s32[768,12]{0,1:T(8,128)} %param.13) | copy-start | bytes 110596
  60.6 86.9 %all-to-all-start.3 = ((bf16[64,72,128]{2,1,0:T(8,128)(2,1)}), bf16[64,72,128]{2,1,0:T(8,128)(2,1)S(1)}, u32[]{:S(2)}, u32[]{:S(2)}) async-start(bf16[64,72,128]{2,1,0:T(8,128)(2,1)} %bitcast.17), calls=%async_computation.3 | async-start | bytes 2359296 | tf_op jit(solution)/shard_map/all_to_all | solution.py:361
  147.5 1.0 copy-start.4
  148.5 88.3 %all-to-all-start.2 = ((bf16[64,72,128]{2,1,0:T(8,128)(2,1)}), bf16[64,72,128]{2,1,0:T(8,128)(2,1)S(1)}, u32[]{:S(2)}, u32[]{:S(2)}) async-start(bf16[64,72,128]{2,1,0:T(8,128)(2,1)} %bitcast.25), calls=%async_computation.2 | async-start | bytes 2359296 | tf_op jit(solution)/shard_map/all_to_all | solution.py:407
  236.9 30.6 %copy-start.2 = (bf16[64,72,128]{2,1,0:T(8,128)(2,1)}, bf16[64,72,128]{2,1,0:T(8,128)(2,1)S(1)}, u32[]{:S(2)}) copy-start(bf16[64,72,128]{2,1,0:T(8,128)(2,1)S(1)} %all-to-all-done.2) | copy-start | bytes 3538948

commit v3 on v2

--- a/solution.py
+++ b/solution.py
@@ -10,6 +10,8 @@
 NEG_BIG = 1000000000.0
 EPSILON = 1e-05
 CHUNKS = 2
+ATTEND_MIB = 40
+TURN_MIB = 60
 TOTAL_LOW = 1e-20
 TOTAL_HIGH = 1e30
 NT = (((1,), (1,)), ((), ()))
@@ -51,8 +53,10 @@
         bias_ref[pl.ds(copy * rows * heads, rows * heads), :] = wide_ref[...].astype(jnp.bfloat16)
 
 
-def layout_kernel(rows, width, groups, chunks, normed_ref, *refs):
-    chunk_refs, wide_ref, staged_refs = refs[:chunks], refs[chunks], refs[chunks + 1 :]
+def layout_kernel(rows, width, groups, chunks, normed_ref, mask_ref, *refs):
+    weight_refs, chunk_refs = refs[:4], refs[4 : 4 + chunks]
+    present_ref, packed_ref, wide_ref = refs[4 + chunks : 7 + chunks]
+    staged_refs = refs[7 + chunks :]
     cols = width // groups
     per = cols // chunks
     for row in range(rows):
@@ -64,6 +68,10 @@
             ]
     for chunk in range(chunks):
         chunk_refs[chunk][...] = staged_refs[chunk][...].astype(jnp.bfloat16)
+    present_ref[...] = mask_ref[...].astype(jnp.float32).T.astype(jnp.bfloat16)
+    channels = normed_ref.shape[1]
+    for at, ref in enumerate(weight_refs):
+        packed_ref[:, at * channels : (at + 1) * channels] = ref[...]
 
 
 def hold_kernel(*refs):
@@ -178,27 +186,19 @@
     heads,
     moved_ref,
     bias_ref,
-    mask_ref,
-    query_weight_ref,
-    key_weight_ref,
-    value_weight_ref,
-    gate_weight_ref,
+    present_ref,
+    weight_ref,
     gate_offset_ref,
     out_ref,
     source_ref,
-    weight_ref,
-    present_ref,
     result_ref,
     fine_ref,
     *sets,
 ):
     channels = moved_ref.shape[1]
-    width, mask_cols = mask_ref.shape
+    width, mask_cols = present_ref.shape
     head_dim = channels // heads
     source_ref[...] = moved_ref[...].astype(jnp.float32)
-    for at, ref in enumerate((query_weight_ref, key_weight_ref, value_weight_ref, gate_weight_ref)):
-        weight_ref[:, at * channels : (at + 1) * channels] = ref[...]
-    present_ref[...] = mask_ref[...].astype(jnp.float32).astype(jnp.bfloat16)
     lane_head = lax.broadcasted_iota(jnp.int32, (1, channels), 1) // head_dim
     own = [(lane_head == head).astype(jnp.bfloat16) for head in range(heads)]
     fine_ref[...] = jnp.ones_like(fine_ref)
@@ -238,15 +238,24 @@
     for part in range(heads):
         project(0, part, first_set)
 
+    def column(col, now, later=None):
+        for head in range(heads):
+            attend(head, now)
+            if later is not None:
+                project(col + 1, head, later)
+        close(col, now)
+
     def two_columns(step, carry):
-        for now, later, col in ((first_set, second_set, 2 * step), (second_set, first_set, 2 * step + 1)):
-            for head in range(heads):
-                attend(head, now)
-                project(jnp.minimum(col + 1, per - 1), head, later)
-            close(col, now)
+        column(2 * step, first_set, second_set)
+        column(2 * step + 1, second_set, first_set)
         return carry
 
-    lax.fori_loop(0, per // 2, two_columns, 0)
+    lax.fori_loop(0, (per - 1) // 2, two_columns, 0)
+    if per % 2 == 0:
+        column(per - 2, first_set, second_set)
+        column(per - 1, second_set)
+    else:
+        column(per - 1, first_set)
 
     @pl.when(jnp.min(fine_ref[...]) < 0.5)
     def _():
@@ -319,7 +328,7 @@
     heads = bias_weight.shape[1]
     block = groups * rows * per
     low, wide = jnp.bfloat16, jnp.float32
-    params = pltpu.CompilerParams(vmem_limit_bytes=56 * 1024 * 1024)
+    params = pltpu.CompilerParams(vmem_limit_bytes=60 * 1024 * 1024)
     normed, bias_copies = pl.pallas_call(
         functools.partial(norm_kernel, rows, width, heads),
         out_shape=[
@@ -332,16 +341,17 @@
         compiler_params=params,
         name="norm",
     )(pair.reshape(rows * width, channels), ln_gain.reshape(1, channels), ln_offset.reshape(1, channels), bias_weight.T)
-    sends = pl.pallas_call(
+    *sends, present, packed = pl.pallas_call(
         functools.partial(layout_kernel, rows, width, groups, CHUNKS),
-        out_shape=[jax.ShapeDtypeStruct((block, channels), low)] * CHUNKS,
-        in_specs=in_vmem(1),
-        out_specs=in_vmem(CHUNKS),
+        out_shape=[jax.ShapeDtypeStruct((block, channels), low)] * CHUNKS
+        + [jax.ShapeDtypeStruct((width, cols), low), jax.ShapeDtypeStruct((channels, 4 * channels), low)],
+        in_specs=in_vmem(6),
+        out_specs=in_vmem(CHUNKS + 2),
         scratch_shapes=[pltpu.VMEM((2, width, channels), wide)] + [pltpu.VMEM((block, channels), wide)] * CHUNKS,
         compiler_params=params,
         cost_estimate=pl.CostEstimate(flops=10**6, bytes_accessed=15 * 10**6, transcendentals=0),
         name="layout",
-    )(normed)
+    )(normed, pair_mask.T, query_weight, key_weight, value_weight, gate_weight)
 
     pieces, sends = gather_bias(bias_copies, sends)
     whole = pl.BlockSpec(memory_space=pl.ANY)
@@ -354,7 +364,7 @@
         out_specs=in_vmem(1) + [whole] * len(later),
         input_output_aliases={len(pieces) + at: 1 + at for at in range(len(later))},
         scratch_shapes=[pltpu.VMEM((width // channels, width * heads, channels), wide)],
-        compiler_params=params,
+        compiler_params=pltpu.CompilerParams(vmem_limit_bytes=TURN_MIB * 1024 * 1024),
         name="turn",
     )(*pieces, *later)
     moved = [
@@ -369,12 +379,10 @@
         gated = pl.pallas_call(
             functools.partial(attend_kernel, chunk, per, heads),
             out_shape=jax.ShapeDtypeStruct((block, channels), low),
-            in_specs=in_vmem(8),
+            in_specs=in_vmem(5),
             out_specs=in_vmem(1)[0],
             scratch_shapes=[
                 pltpu.VMEM((block, channels), wide),
-                pltpu.VMEM((channels, 4 * channels), low),
-                pltpu.VMEM(pair_mask.shape, low),
                 pltpu.VMEM((block, channels), wide),
                 pltpu.VMEM((8, channels), wide),
             ]
@@ -386,7 +394,7 @@
                 pltpu.VMEM((width, channels), low),
                 pltpu.VMEM((width, 2 * channels), wide),
             ],
-            compiler_params=params,
+            compiler_params=pltpu.CompilerParams(vmem_limit_bytes=ATTEND_MIB * 1024 * 1024),
             cost_estimate=pl.CostEstimate(
                 flops=per * heads * width * width * channels * 6,
                 bytes_accessed=2 * heads * width * width,
@@ -396,11 +404,8 @@
         )(
             moved[chunk],
             turned,
-            pair_mask,
-            query_weight,
-            key_weight,
-            value_weight,
-            gate_weight,
+            present,
+            packed,
             gate_offset.reshape(1, channels),
         )
         returned.append(

time: 273 us -> 282 us (1.033); the launches traced: 272 us -> 277 us
  Pallas kernels: 178 us -> 171 us
  starting transfers between devices: 45.1 us -> 50.5 us
  waiting for transfers between devices: 14.2 us -> 18.9 us
    all_to_all x1, starting transfers between devices: 10.4 us -> 19.3 us  [local(): lax.all_to_all(gated.reshape(groups, rows * per, channels), 'dap', split_...]
    pallas_call x2, Pallas kernels: 156 us -> 149 us  [local(): pl.pallas_call(functools.partial(attend_kernel, chunk, per, heads), out_s...]
    ppermute x3, waiting for transfers between devices: 6.95 us -> 11.7 us  [gather_bias(): lax.ppermute(first, 'dap', second_pairs(step))]
    unnamed x27 -> x28, local copies, waits for them, and re-layouts: 4.61 us -> 6.31 us
  transfers between devices with their start and end apart: 11 -> 11, of which waited for: 3 -> 4; matrix products, arithmetic and copies ran while one was open for 0% -> 0% of each run, Pallas kernels for 61% -> 58%
where the time goes in v3:
time: 282 us; the launch traced here: 277 us
  Pallas kernels  171 us (61%)
  starting transfers between devices  50.5 us (18%)
  blocking collectives  30.4 us (11%)
  waiting for transfers between devices  18.9 us (7%)
  local copies, waits for them, and re-layouts  6.31 us (2%)
    pallas_call x2, Pallas kernels, local(): pl.pallas_call(functools.partial(attend_kernel, chunk, per, heads), out_s...  149 us
    all_to_all x1, blocking collectives, local(): lax.all_to_all(gated.reshape(groups, rows * per, channels), 'dap', split_...  30.4 us
    all_to_all x1, starting transfers between devices, local(): lax.all_to_all(gated.reshape(groups, rows * per, channels), 'dap', split_...  19.3 us
    all_to_all x2, starting transfers between devices, local(): lax.all_to_all(send.reshape(groups, rows * per, channels), 'dap', split_a...  15.1 us
    ppermute x3, waiting for transfers between devices, gather_bias(): lax.ppermute(first, 'dap', second_pairs(step))  11.7 us
    all_to_all x1, starting transfers between devices, gather_bias(): lax.all_to_all(bias_copies.reshape((FIRST, bias_copies.shape[0] // FIRST,...  8.16 us
    pallas_call x1, Pallas kernels, local(): pl.pallas_call(functools.partial(turn_kernel, heads, rows, len(later)), o...  6.49 us
    unnamed x28, local copies, waits for them, and re-layouts  6.31 us
  transfers between devices with their start and end apart: 11, of which 4 were waited for; matrix products, arithmetic and copies ran while one was open for 0% of the time, Pallas kernels for 58%

profile of v3, /device:TPU:1, one launch (start us, length us, event | category | flops | bytes accessed | tf_op | source)
XLA Modules:
  0.0 277.1 jit_solution(16081844861058571832)
XLA Ops:
  0.0 6.0 %norm.1 = (bf16[9216,128]{1,0:T(8,128)(2,1)}, bf16[384,768]{1,0:T(8,128)(2,1)}) custom-call(bf16[9216,128]{1,0:T(8,128)(2,1)} %bitcast.27, f32[1,128]{1,0:T(1,128)} %bitcast.32, f32[1,128]{1,0:T(1,128)} %bitcast.33, bf16[4,128]{1,0:T(4,128)(2,1)} %bitcast.30), custom_call_target="tpu_custom_call" | custom-call | tf_op jit(solution)/shard_map/norm/pallas_call | solution.py:332
  6.0 8.2 %all-to-all-start = ((bf16[8,48,768]{2,1,0:T(8,128)(2,1)}), bf16[8,48,768]{2,1,0:T(8,128)(2,1)S(1)}, u32[]{:S(2)}, u32[]{:S(2)}) async-start(bf16[8,48,768]{2,1,0:T(8,128)(2,1)} %bitcast.28), calls=%async_computation | async-start | bytes 1179648 | tf_op jit(solution)/shard_map/all_to_all | solution.py:129
  14.1 4.5 %layout.1 = (bf16[4608,128]{1,0:T(8,128)(2,1)}, bf16[4608,128]{1,0:T(8,128)(2,1)}, bf16[768,12]{1,0:T(8,128)(2,1)}, bf16[128,512]{1,0:T(8,128)(2,1)}) custom-call(bf16[9216,128]{1,0:T(8,128)(2,1)} %get-tuple-element.17.normed_ref, s32[12,768]{1,0:T(8,128)} %bitcast.29, bf16[128,128]{1,0:T(8,128)(2,1)} %refs_0_.1, bf16[128,128]{1,0:T(8,128)(2,1)} %refs_1_.1, ...), custom_call_target="tpu_custom_call" | custom-call | flops 1000000 | bytes 15000000 | tf_op jit(solution)/shard_map/layout/pallas_call | solution.py:344
  18.7 5.6 %all-to-all-done = bf16[8,48,768]{2,1,0:T(8,128)(2,1)S(1)} async-done(((bf16[8,48,768]{2,1,0:T(8,128)(2,1)}), bf16[8,48,768]{2,1,0:T(8,128)(2,1)S(1)}, u32[]{:S(2)}, u32[]{:S(2)}) %all-to-all-start) | async-done | bytes 589856 | tf_op jit(solution)/shard_map/all_to_all | solution.py:129
  24.3 0.0 copy-start.5
  24.3 0.8 copy-done.5
  25.1 3.0 %collective-permute-start.2 = (bf16[384,768]{1,0:T(8,128)(2,1)}, bf16[384,768]{1,0:T(8,128)(2,1)S(1)}, u32[]{:S(2)}, u32[]{:S(2)}) collective-permute-start(bf16[384,768]{1,0:T(8,128)(2,1)} %get-tuple-element.21.refs_0_), channel_id=1, source_target_pairs={{0,12},{2,50},{4,0},{6,54},{8,4},{10,58},{12,8},{14,62},{16,28},{1... | collective-permute-start | bytes 1769480 | tf_op jit(solution)/shard_map/ppermute | solution.py:138
  28.1 0.2 collective-permute-start.1
  28.4 0.7 collective-permute-start
  29.1 0.0 copy-start.6
  29.1 9.0 %all-to-all-start.1 = ((bf16[64,72,128]{2,1,0:T(8,128)(2,1)}), bf16[64,72,128]{2,1,0:T(8,128)(2,1)S(1)}, u32[]{:S(2)}, u32[]{:S(2)}) async-start(bf16[64,72,128]{2,1,0:T(8,128)(2,1)} %bitcast.26), calls=%async_computation.1 | async-start | bytes 2359296 | tf_op jit(solution)/shard_map/all_to_all | solution.py:371
  38.1 0.0 copy-done.6
  38.1 0.5 collective-permute-start.3
  38.6 7.2 %collective-permute-done.2.refs_3_ = bf16[384,768]{1,0:T(8,128)(2,1)S(1)} collective-permute-done((bf16[384,768]{1,0:T(8,128)(2,1)}, bf16[384,768]{1,0:T(8,128)(2,1)S(1)}, u32[]{:S(2)}, u32[]{:S(2)}) %collective-permute-start.2) | collective-permute-done | bytes 589856 | tf_op jit(solution)/shard_map/ppermute | solution.py:138
  45.8 0.0 copy-start.7
  45.8 0.0 collective-permute-start.6
  45.8 0.0 collective-permute-done.1.refs_2_
  45.8 0.0 copy-start.8
  45.8 0.5 collective-permute-start.5
  46.3 4.5 %collective-permute-done.refs_1_ = bf16[384,768]{1,0:T(8,128)(2,1)S(1)} collective-permute-done((bf16[384,768]{1,0:T(8,128)(2,1)}, bf16[384,768]{1,0:T(8,128)(2,1)S(1)}, u32[]{:S(2)}, u32[]{:S(2)}) %collective-permute-start) | collective-permute-done | bytes 589856 | tf_op jit(solution)/shard_map/ppermute | solution.py:138
  50.8 0.0 copy-start.9
  50.8 3.0 %collective-permute-start.4 = (bf16[384,768]{1,0:T(8,128)(2,1)S(1)}, bf16[384,768]{1,0:T(8,128)(2,1)S(1)}, u32[]{:S(2)}, u32[]{:S(2)}) collective-permute-start(bf16[384,768]{1,0:T(8,128)(2,1)S(1)} %collective-permute-done.refs_1_), channel_id=1, source_target_pairs={{0,2},{2,0},{4,6},{6,4},{8,10},{10,8},{12,14},{14,12},{16,18},{18,... | collective-permute-start | bytes 1769480 | tf_op jit(solution)/shard_map/ppermute | solution.py:140
  53.8 0.0 collective-permute-done.3.refs_4_
  53.8 0.0 copy-start.10
  53.8 0.0 collective-permute-done.6.refs_7_
  53.8 0.0 copy-start.11
  53.8 0.0 collective-permute-done.5.refs_6_
  53.9 0.0 copy-start.12
  53.9 1.6 collective-permute-done.4.refs_5_
  55.5 0.0 copy-done.10
  55.5 0.0 copy-done.11
  55.5 0.0 copy-done.12
  55.5 0.0 copy-start.13
  55.5 0.8 copy-done.13
  56.3 0.0 copy-done.7
  56.3 0.0 copy-done.8
  56.3 0.0 copy-done.9
  56.3 6.5 %turn.1 = (bf16[4,768,768]{2,1,0:T(8,128)(2,1)}, bf16[4608,128]{1,0:T(8,128)(2,1)}) custom-call(bf16[384,768]{1,0:T(8,128)(2,1)} %get-tuple-element.21.refs_0_, bf16[384,768]{1,0:T(8,128)(2,1)} %copy-done.9, bf16[384,768]{1,0:T(8,128)(2,1)} %copy-done.8, bf16[384,768]{1,0:T(8,128)(2,1)} %copy-done.7, ...), custom_call_target="tpu_custom_call", output_to_operand_aliasing={{1}: (8, {})} | custom-call | tf_op jit(solution)/shard_map/turn/pallas_call | solution.py:359
  62.8 0.0 all-to-all-done.1
  62.8 0.0 copy-start.2
  62.8 0.0 copy-start.3
  62.8 0.0 copy-start.4
  62.8 6.1 %all-to-all-start.3 = ((bf16[64,72,128]{2,1,0:T(8,128)(2,1)}), bf16[64,72,128]{2,1,0:T(8,128)(2,1)S(1)}, u32[]{:S(2)}, u32[]{:S(2)}) async-start(bf16[64,72,128]{2,1,0:T(8,128)(2,1)} %bitcast.23), calls=%async_computation.3 | async-start | bytes 2359296 | tf_op jit(solution)/shard_map/all_to_all | solution.py:371
  68.9 0.0 copy-done.2
  68.9 0.0 copy-done.3
  69.0 0.0 copy-done.4
  69.0 0.0 copy-start
  69.0 2.3 copy-done
  71.3 74.8 %attend.2 = bf16[4608,128]{1,0:T(8,128)(2,1)} custom-call(bf16[4608,128]{1,0:T(8,128)(2,1)S(1)} %bitcast.18, bf16[4,768,768]{2,1,0:T(8,128)(2,1)S(1)} %copy-done, bf16[768,12]{1,0:T(8,128)(2,1)S(1)} %copy-done.2, bf16[128,512]{1,0:T(8,128)(2,1)S(1)} %copy-done.3, f32[1,128]{1,0:T(1,128)S(1)} %bitcast.21), custom_call_target="tpu_custom_call" | custom-call | flops 10871635968 | bytes 4718592 | tf_op jit(solution)/shard_map/attend/pallas_call | solution.py:379
  146.1 0.0 all-to-all-done.3
  146.1 19.3 %all-to-all-start.2 = ((bf16[64,72,128]{2,1,0:T(8,128)(2,1)}), bf16[64,72,128]{2,1,0:T(8,128)(2,1)}, u32[]{:S(2)}, u32[]{:S(2)}) async-start(bf16[64,72,128]{2,1,0:T(8,128)(2,1)} %bitcast.10), calls=%async_computation.2 | async-start | bytes 2359296 | tf_op jit(solution)/shard_map/all_to_all | solution.py:412
  165.3 0.0 copy-start.1
  165.4 2.3 copy-done.1
  167.7 74.0 %attend.3 = bf16[4608,128]{1,0:T(8,128)(2,1)S(1)} custom-call(bf16[4608,128]{1,0:T(8,128)(2,1)S(1)} %bitcast.19, bf16[4,768,768]{2,1,0:T(8,128)(2,1)S(1)} %copy-done.1, bf16[768,12]{1,0:T(8,128)(2,1)S(1)} %copy-done.2, bf16[128,512]{1,0:T(8,128)(2,1)S(1)} %copy-done.3, f32[1,128]{1,0:T(1,128)S(1)} %bitcast.22), custom_call_target="tpu_custom_call" | custom-call | flops 10871635968 | bytes 4718592 | tf_op jit(solution)/shard_map/attend/pallas_call | solution.py:379
  241.7 0.0 all-to-all-done.2
  241.7 30.4 %all_to_all.25 = bf16[64,72,128]{2,1,0:T(8,128)(2,1)} all-to-all(bf16[64,72,128]{2,1,0:T(8,128)(2,1)S(1)} %bitcast.20), channel_id=1, replica_groups=mesh['dap'=64,'dp'=2] {'dap'}, dimensions={0} | all-to-all | bytes 2359296 | tf_op jit(solution)/shard_map/all_to_all | solution.py:412
  272.1 4.8 %finish.1 = bf16[9216,128]{1,0:T(8,128)(2,1)} custom-call(bf16[4608,128]{1,0:T(8,128)(2,1)} %bitcast.11.refs_0_, bf16[4608,128]{1,0:T(8,128)(2,1)} %bitcast.25, bf16[128,128]{1,0:T(8,128)(2,1)} %refs_2_.3, f32[1,128]{1,0:T(1,128)} %bitcast.31), custom_call_target="tpu_custom_call" | custom-call | tf_op jit(solution)/shard_map/finish/pallas_call | solution.py:416
  (1 shorter events, 0.0 us)
Async XLA Ops:
  6.0 18.3 %all-to-all-start = ((bf16[8,48,768]{2,1,0:T(8,128)(2,1)}), bf16[8,48,768]{2,1,0:T(8,128)(2,1)S(1)}, u32[]{:S(2)}, u32[]{:S(2)}) async-start(bf16[8,48,768]{2,1,0:T(8,128)(2,1)} %bitcast.28), calls=%async_computation | async-start | bytes 1179648 | tf_op jit(solution)/shard_map/all_to_all | solution.py:129
  24.3 0.8 copy-start.5
  25.1 20.6 %collective-permute-start.2 = (bf16[384,768]{1,0:T(8,128)(2,1)}, bf16[384,768]{1,0:T(8,128)(2,1)S(1)}, u32[]{:S(2)}, u32[]{:S(2)}) collective-permute-start(bf16[384,768]{1,0:T(8,128)(2,1)} %get-tuple-element.21.refs_0_), channel_id=1, source_target_pairs={{0,12},{2,50},{4,0},{6,54},{8,4},{10,58},{12,8},{14,62},{16,28},{1... | collective-permute-start | bytes 1769480 | tf_op jit(solution)/shard_map/ppermute | solution.py:138
  28.1 17.6 %collective-permute-start.1 = (bf16[384,768]{1,0:T(8,128)(2,1)}, bf16[384,768]{1,0:T(8,128)(2,1)S(1)}, u32[]{:S(2)}, u32[]{:S(2)}) collective-permute-start(bf16[384,768]{1,0:T(8,128)(2,1)} %get-tuple-element.21.refs_0_), channel_id=1, source_target_pairs={{0,8},{2,34},{4,12},{6,38},{8,0},{10,42},{12,4},{14,46},{16,24},{1... | collective-permute-start | bytes 1769480 | tf_op jit(solution)/shard_map/ppermute | solution.py:138
  28.4 22.4 %collective-permute-start = (bf16[384,768]{1,0:T(8,128)(2,1)}, bf16[384,768]{1,0:T(8,128)(2,1)S(1)}, u32[]{:S(2)}, u32[]{:S(2)}) collective-permute-start(bf16[384,768]{1,0:T(8,128)(2,1)} %get-tuple-element.21.refs_0_), channel_id=1, source_target_pairs={{0,4},{2,18},{4,8},{6,22},{8,12},{10,26},{12,0},{14,30},{16,20},{1... | collective-permute-start | bytes 1769480 | tf_op jit(solution)/shard_map/ppermute | solution.py:138
  29.1 9.0 %copy-start.6 = (bf16[384,768]{1,0:T(8,128)(2,1)S(1)}, bf16[384,768]{1,0:T(8,128)(2,1)}, u32[]{:S(2)}) copy-start(bf16[384,768]{1,0:T(8,128)(2,1)} %get-tuple-element.21.refs_0_) | copy-start | bytes 1769476
  29.1 33.7 %all-to-all-start.1 = ((bf16[64,72,128]{2,1,0:T(8,128)(2,1)}), bf16[64,72,128]{2,1,0:T(8,128)(2,1)S(1)}, u32[]{:S(2)}, u32[]{:S(2)}) async-start(bf16[64,72,128]{2,1,0:T(8,128)(2,1)} %bitcast.26), calls=%async_computation.1 | async-start | bytes 2359296 | tf_op jit(solution)/shard_map/all_to_all | solution.py:371
  38.1 15.8 %collective-permute-start.3 = (bf16[384,768]{1,0:T(8,128)(2,1)S(1)}, bf16[384,768]{1,0:T(8,128)(2,1)S(1)}, u32[]{:S(2)}, u32[]{:S(2)}) collective-permute-start(bf16[384,768]{1,0:T(8,128)(2,1)S(1)} %copy-done.6), channel_id=1, source_target_pairs={{0,2},{2,0},{4,6},{6,4},{8,10},{10,8},{12,14},{14,12},{16,18},{18,... | collective-permute-start | bytes 1769480 | tf_op jit(solution)/shard_map/ppermute | solution.py:140
  45.8 10.5 %copy-start.7 = (bf16[384,768]{1,0:T(8,128)(2,1)}, bf16[384,768]{1,0:T(8,128)(2,1)S(1)}, u32[]{:S(2)}) copy-start(bf16[384,768]{1,0:T(8,128)(2,1)S(1)} %collective-permute-done.2.refs_3_) | copy-start | bytes 1769476
  45.8 8.1 %collective-permute-start.6 = (bf16[384,768]{1,0:T(8,128)(2,1)S(1)}, bf16[384,768]{1,0:T(8,128)(2,1)S(1)}, u32[]{:S(2)}, u32[]{:S(2)}) collective-permute-start(bf16[384,768]{1,0:T(8,128)(2,1)S(1)} %collective-permute-done.2.refs_3_), channel_id=1, source_target_pairs={{0,2},{2,0},{4,6},{6,4},{8,10},{10,8},{12,14},{14,12},{16,18},{18,... | collective-permute-start | bytes 1769480 | tf_op jit(solution)/shard_map/ppermute | solution.py:140
  45.8 10.5 %copy-start.8 = (bf16[384,768]{1,0:T(8,128)(2,1)}, bf16[384,768]{1,0:T(8,128)(2,1)S(1)}, u32[]{:S(2)}) copy-start(bf16[384,768]{1,0:T(8,128)(2,1)S(1)} %collective-permute-done.1.refs_2_) | copy-start | bytes 1769476
  45.8 8.1 %collective-permute-start.5 = (bf16[384,768]{1,0:T(8,128)(2,1)S(1)}, bf16[384,768]{1,0:T(8,128)(2,1)S(1)}, u32[]{:S(2)}, u32[]{:S(2)}) collective-permute-start(bf16[384,768]{1,0:T(8,128)(2,1)S(1)} %collective-permute-done.1.refs_2_), channel_id=1, source_target_pairs={{0,2},{2,0},{4,6},{6,4},{8,10},{10,8},{12,14},{14,12},{16,18},{18,... | collective-permute-start | bytes 1769480 | tf_op jit(solution)/shard_map/ppermute | solution.py:140
  50.8 5.5 %copy-start.9 = (bf16[384,768]{1,0:T(8,128)(2,1)}, bf16[384,768]{1,0:T(8,128)(2,1)S(1)}, u32[]{:S(2)}) copy-start(bf16[384,768]{1,0:T(8,128)(2,1)S(1)} %collective-permute-done.refs_1_) | copy-start | bytes 1769476
  50.8 4.6 %collective-permute-start.4 = (bf16[384,768]{1,0:T(8,128)(2,1)S(1)}, bf16[384,768]{1,0:T(8,128)(2,1)S(1)}, u32[]{:S(2)}, u32[]{:S(2)}) collective-permute-start(bf16[384,768]{1,0:T(8,128)(2,1)S(1)} %collective-permute-done.refs_1_), channel_id=1, source_target_pairs={{0,2},{2,0},{4,6},{6,4},{8,10},{10,8},{12,14},{14,12},{16,18},{18,... | collective-permute-start | bytes 1769480 | tf_op jit(solution)/shard_map/ppermute | solution.py:140
  53.8 1.6 copy-start.10
  53.8 1.6 copy-start.11
  53.9 1.6 copy-start.12
  55.5 0.8 copy-start.13
  62.8 6.2 %copy-start.2 = (bf16[768,12]{1,0:T(8,128)(2,1)S(1)}, bf16[768,12]{1,0:T(8,128)(2,1)}, u32[]{:S(2)}) copy-start(bf16[768,12]{1,0:T(8,128)(2,1)} %get-tuple-element.24.present_ref) | copy-start | bytes 55300
  62.8 6.2 %copy-start.3 = (bf16[128,512]{1,0:T(8,128)(2,1)S(1)}, bf16[128,512]{1,0:T(8,128)(2,1)}, u32[]{:S(2)}) copy-start(bf16[128,512]{1,0:T(8,128)(2,1)} %get-tuple-element.25.weight_ref) | copy-start | bytes 393220
  62.8 6.2 %copy-start.4 = (f32[128]{0:T(128)S(1)}, f32[128]{0:T(128)}, u32[]{:S(2)}) copy-start(f32[128]{0:T(128)} %param.21) | copy-start | bytes 1540
  62.8 83.3 %all-to-all-start.3 = ((bf16[64,72,128]{2,1,0:T(8,128)(2,1)}), bf16[64,72,128]{2,1,0:T(8,128)(2,1)S(1)}, u32[]{:S(2)}, u32[]{:S(2)}) async-start(bf16[64,72,128]{2,1,0:T(8,128)(2,1)} %bitcast.23), calls=%async_computation.3 | async-start | bytes 2359296 | tf_op jit(solution)/shard_map/all_to_all | solution.py:371
  69.0 2.3 copy-start
  146.1 95.6 %all-to-all-start.2 = ((bf16[64,72,128]{2,1,0:T(8,128)(2,1)}), bf16[64,72,128]{2,1,0:T(8,128)(2,1)}, u32[]{:S(2)}, u32[]{:S(2)}) async-start(bf16[64,72,128]{2,1,0:T(8,128)(2,1)} %bitcast.10), calls=%async_computation.2 | async-start | bytes 2359296 | tf_op jit(solution)/shard_map/all_to_all | solution.py:412
  165.3 2.3 copy-start.1
